TPU v7x, 256 devices: a whole 4x4x8 slice. The times are simulated.
256 devices in a mesh: dom: 128 (over z, x, y_hi, core), col: 2 (over y_lo).
Axes of the slice: x: 4, y: 4 (y_hi: 2, y_lo: 2; y = y_hi * 2 + y_lo), z: 8, core: 2. Of those that a mesh axis runs over, the one named last changes fastest.
Arguments:
- density: bfloat16 [2, 768, 4, 128, 128], P(None, 'dom', 'col'), may hold values from -6 to 6
- hamiltonian: bfloat16 [768, 4, 128, 128], P('dom', 'col'), may hold values from -0.25 to 0.25
- neighbours: int32 [768, 4], P('dom'), may hold values from 0 to 767, as said below
Outputs:
- evolved: float32 [2, 768, 4, 128, 128], P(None, 'dom', 'col')
Inputs may be any that keep to these rules, and one draw needn't show every extreme that they name: `neighbours`: each block row lists 4 different block rows, itself among them, none more than 3 rows away from it, in a drawn order of slots.
All inputs are finite; a program needn't handle non-finite values.
Results may differ from a plain program's by a relative error of at most 0.004.
Values may be sent and summed in bfloat16 or wider, within the bound.
No kernel may reach another device: no remote copies, remote signals or barrier semaphores. Data moves between devices by JAX's collectives and lax.ppermute only.
A program may use at most 64 MiB of HBM per device.

v0:
```python
import jax
import jax.numpy as jnp
from jax import lax
from jax.sharding import PartitionSpec as P

STEPS = 2
ORDERS = 4
REACH = 3


def padded(cells, sides, width):
    for axis, dim in sides:
        count = lax.axis_size(axis)
        ends = count - 1
        head = lax.slice_in_dim(cells, 0, width, axis=dim)
        tail = lax.slice_in_dim(cells, cells.shape[dim] - width, cells.shape[dim], axis=dim)
        cells = jnp.concatenate(
            [
                lax.ppermute(tail, axis, [(i, (i + 1) % count) for i in range(ends)]),
                cells,
                lax.ppermute(head, axis, [((i + 1) % count, i) for i in range(ends)]),
            ],
            axis=dim,
        )
    return cells


def shards(density, hamiltonian, neighbours):
    row_count = neighbours.shape[0]
    slot_count = neighbours.shape[1]
    own_slots = density.shape[2]
    block_size = density.shape[3]
    domain_index = lax.axis_index("dom")
    column_index = lax.axis_index("col")
    wide_pattern = padded(neighbours, (("dom", 0),), REACH)
    offset = domain_index * row_count - REACH
    local_rows = neighbours - offset
    rows_of = jnp.take(wide_pattern, local_rows, axis=0)
    targets = lax.dynamic_slice_in_dim(neighbours, column_index * own_slots, own_slots, 1)
    matches = rows_of[:, None, :, :] == targets[:, :, None, None]
    present = jnp.any(matches, axis=-1)
    slot_match = jnp.sum(jnp.where(matches, jnp.arange(slot_count, dtype=jnp.int32), 0), axis=-1)
    wide_count = (row_count + 2 * REACH) * slot_count
    flat_index = jnp.where(present, local_rows[:, None, :] * slot_count + slot_match, wide_count)
    operator_rows = lax.all_gather(hamiltonian, "col", axis=1, tiled=True)
    operator_wide = padded(operator_rows, (("dom", 0),), REACH)
    zero_block = jnp.zeros((1, block_size, block_size), jnp.bfloat16)
    operator_flat = jnp.concatenate(
        [operator_wide.reshape(-1, block_size, block_size), zero_block], axis=0
    )
    picked_operator = jnp.take(operator_flat, flat_index, axis=0)
    operator_joined = jnp.transpose(operator_rows, (0, 2, 1, 3)).reshape(
        row_count, block_size, slot_count * block_size
    )
    series_term = density
    running_sum = series_term.astype(jnp.float32)
    for time_step in range(STEPS):
        running_sum = series_term.astype(jnp.float32)
        for series_order in range(1, ORDERS + 1):
            term_rows = lax.all_gather(series_term, "col", axis=2, tiled=True)
            term_wide = padded(term_rows, (("dom", 1),), REACH)
            zero_pair = jnp.zeros((2, 1, block_size, block_size), jnp.bfloat16)
            term_flat = jnp.concatenate(
                [term_wide.reshape(2, -1, block_size, block_size), zero_pair], axis=1
            )
            picked_term = jnp.take(term_flat, flat_index, axis=1)
            picked_joined = picked_term.reshape(
                2, row_count, own_slots, slot_count * block_size, block_size
            )
            left_product = jnp.einsum(
                "rak,zrskc->zrsac",
                operator_joined,
                picked_joined,
                preferred_element_type=jnp.float32,
            )
            right_product = jnp.einsum(
                "zrtab,rstbc->zrsac", term_rows, picked_operator, preferred_element_type=jnp.float32
            )
            bracket = left_product - right_product
            series_term = (jnp.stack([bracket[1], -bracket[0]]) / series_order).astype(jnp.bfloat16)
            series_term = lax.optimization_barrier(series_term)
            running_sum = running_sum + series_term.astype(jnp.float32)
        if time_step + 1 < STEPS:
            series_term = lax.optimization_barrier(running_sum.astype(jnp.bfloat16))
    return running_sum


def solution(mesh):
    placed = (P(None, "dom", "col", None, None), P("dom", "col", None, None), P("dom", None))
    return jax.shard_map(
        shards,
        mesh=mesh,
        in_specs=placed,
        out_specs=P(None, "dom", "col", None, None),
        check_vma=False,
    )
```

profile of v0, /device:TPU:129, one launch (start us, length us, event | category | flops | bytes accessed | tf_op | source)
XLA Modules:
  0.0 678.7 jit_solution(3023771522919516912)
XLA Ops:
  7.4 5.4 collective-permute-start.2
  16.9 7.3 %all_gather.28 = bf16[6,4,128,128]{3,2,1,0:T(8,128)(2,1)S(1)} all-gather(bf16[6,2,128,128]{3,2,1,0:T(8,128)(2,1)S(1)} %copy-done.24), channel_id=1, replica_groups=mesh['dom'=128,'col'=2] {'col'}, dimensions={1}, use_global_device_ids=true | all-gather | bytes 1179648 | tf_op jit(solution)/shard_map/all_gather | solution.py:45
  24.2 8.1 %collective-permute-start.4 = (bf16[3,4,128,128]{3,2,1,0:T(8,128)(2,1)S(1)}, bf16[3,4,128,128]{3,2,1,0:T(8,128)(2,1)S(1)}, u32[]{:S(2)}, u32[]{:S(2)}) collective-permute-start(bf16[3,4,128,128]{3,2,1,0:T(8,128)(2,1)S(1)} %get-tuple-element.38), channel_id=1, source_target_pairs={{0,2},{2,4},{4,6},{6,8},{8,10},{10,12},{12,14},{14,16},{16,18},{18... | collective-permute-start | bytes 1179656 | tf_op jit(solution)/shard_map/ppermute | solution.py:19
  37.5 21.6 %all-gather.9.cloned.1.call-done = bf16[2,6,4,128,128]{4,3,2,0,1:T(8,128)(2,1)} async-done(((bf16[2,6,2,128,128]{4,3,2,0,1:T(8,128)(2,1)}), bf16[2,6,4,128,128]{4,3,2,0,1:T(8,128)(2,1)}) %all-gather.9.cloned.1.call-update) | async-done | bytes 1572880 | tf_op jit(solution)/shard_map/all_gather | solution.py:60
  73.6 10.8 %collective-permute-done = bf16[2,3,4,128,128]{4,3,2,0,1:T(8,128)(2,1)} collective-permute-done((bf16[2,3,4,128,128]{4,3,2,0,1:T(8,128)(2,1)}, bf16[2,3,4,128,128]{4,3,2,0,1:T(8,128)(2,1)}, u32[]{:S(2)}, u32[]{:S(2)}) %collective-permute-start) | collective-permute-done | bytes 786464 | tf_op jit(solution)/shard_map/ppermute | solution.py:19
  84.4 5.2 collective-permute-done.1
  104.7 29.2 %all-gather.11.cloned.1.call-done = bf16[2,6,4,128,128]{3,4,2,0,1:T(8,128)(2,1)} async-done(((bf16[2,6,2,128,128]{3,4,2,0,1:T(8,128)(2,1)}), bf16[2,6,4,128,128]{3,4,2,0,1:T(8,128)(2,1)}) %all-gather.11.cloned.1.call-update) | async-done | bytes 1572880 | tf_op jit(solution)/shard_map/all_gather | solution.py:60
  135.6 4.9 collective-permute-start.6
  142.4 15.4 %collective-permute-done.6 = bf16[2,3,4,128,128]{3,4,2,0,1:T(8,128)(2,1)S(1)} collective-permute-done((bf16[2,3,4,128,128]{3,4,2,0,1:T(8,128)(2,1)S(1)}, bf16[2,3,4,128,128]{3,4,2,0,1:T(8,128)(2,1)S(1)}, u32[]{:S(2)}, u32[]{:S(2)}) %collective-permute-start.6) | collective-permute-done | bytes 786464 | tf_op jit(solution)/shard_map/ppermute | solution.py:19
  157.8 5.2 collective-permute-done.7
  184.6 29.2 %all-gather.13.cloned.1.call-done = bf16[2,6,4,128,128]{3,4,2,0,1:T(8,128)(2,1)} async-done(((bf16[2,6,2,128,128]{3,4,2,0,1:T(8,128)(2,1)}), bf16[2,6,4,128,128]{3,4,2,0,1:T(8,128)(2,1)}) %all-gather.13.cloned.1.call-update) | async-done | bytes 1572880 | tf_op jit(solution)/shard_map/all_gather | solution.py:60
  215.5 4.9 collective-permute-start.8
  222.8 14.9 %collective-permute-done.8 = bf16[2,3,4,128,128]{3,4,2,0,1:T(8,128)(2,1)S(1)} collective-permute-done((bf16[2,3,4,128,128]{3,4,2,0,1:T(8,128)(2,1)S(1)}, bf16[2,3,4,128,128]{3,4,2,0,1:T(8,128)(2,1)S(1)}, u32[]{:S(2)}, u32[]{:S(2)}) %collective-permute-start.8) | collective-permute-done | bytes 786464 | tf_op jit(solution)/shard_map/ppermute | solution.py:19
  237.8 5.2 collective-permute-done.9
  264.5 29.2 %all-gather.15.cloned.1.call-done = bf16[2,6,4,128,128]{3,4,2,0,1:T(8,128)(2,1)} async-done(((bf16[2,6,2,128,128]{3,4,2,0,1:T(8,128)(2,1)}), bf16[2,6,4,128,128]{3,4,2,0,1:T(8,128)(2,1)}) %all-gather.15.cloned.1.call-update) | async-done | bytes 1572880 | tf_op jit(solution)/shard_map/all_gather | solution.py:60
  296.4 5.0 collective-permute-start.10
  305.7 13.4 %collective-permute-done.10 = bf16[2,3,4,128,128]{3,4,2,0,1:T(8,128)(2,1)} collective-permute-done((bf16[2,3,4,128,128]{3,4,2,0,1:T(8,128)(2,1)}, bf16[2,3,4,128,128]{3,4,2,0,1:T(8,128)(2,1)}, u32[]{:S(2)}, u32[]{:S(2)}) %collective-permute-start.10) | collective-permute-done | bytes 786464 | tf_op jit(solution)/shard_map/ppermute | solution.py:19
  319.1 5.2 collective-permute-done.11
  349.2 29.2 %all-gather.17.cloned.1.call-done = bf16[2,6,4,128,128]{3,4,2,0,1:T(8,128)(2,1)} async-done(((bf16[2,6,2,128,128]{3,4,2,0,1:T(8,128)(2,1)}), bf16[2,6,4,128,128]{3,4,2,0,1:T(8,128)(2,1)}) %all-gather.17.cloned.1.call-update) | async-done | bytes 1572880 | tf_op jit(solution)/shard_map/all_gather | solution.py:60
  380.1 4.9 collective-permute-start.12
  387.1 15.2 %collective-permute-done.12 = bf16[2,3,4,128,128]{3,4,2,0,1:T(8,128)(2,1)S(1)} collective-permute-done((bf16[2,3,4,128,128]{3,4,2,0,1:T(8,128)(2,1)S(1)}, bf16[2,3,4,128,128]{3,4,2,0,1:T(8,128)(2,1)S(1)}, u32[]{:S(2)}, u32[]{:S(2)}) %collective-permute-start.12) | collective-permute-done | bytes 786464 | tf_op jit(solution)/shard_map/ppermute | solution.py:19
  402.3 5.2 collective-permute-done.13
  429.1 29.2 %all-gather.19.cloned.1.call-done = bf16[2,6,4,128,128]{3,4,2,0,1:T(8,128)(2,1)} async-done(((bf16[2,6,2,128,128]{3,4,2,0,1:T(8,128)(2,1)}), bf16[2,6,4,128,128]{3,4,2,0,1:T(8,128)(2,1)}) %all-gather.19.cloned.1.call-update) | async-done | bytes 1572880 | tf_op jit(solution)/shard_map/all_gather | solution.py:60
  466.8 15.4 %collective-permute-done.14 = bf16[2,3,4,128,128]{3,4,2,0,1:T(8,128)(2,1)S(1)} collective-permute-done((bf16[2,3,4,128,128]{3,4,2,0,1:T(8,128)(2,1)S(1)}, bf16[2,3,4,128,128]{3,4,2,0,1:T(8,128)(2,1)S(1)}, u32[]{:S(2)}, u32[]{:S(2)}) %collective-permute-start.14) | collective-permute-done | bytes 786464 | tf_op jit(solution)/shard_map/ppermute | solution.py:19
  482.2 5.2 collective-permute-done.15
  508.9 29.2 %all-gather.21.cloned.1.call-done = bf16[2,6,4,128,128]{3,4,2,0,1:T(8,128)(2,1)} async-done(((bf16[2,6,2,128,128]{3,4,2,0,1:T(8,128)(2,1)}), bf16[2,6,4,128,128]{3,4,2,0,1:T(8,128)(2,1)}) %all-gather.21.cloned.1.call-update) | async-done | bytes 1572880 | tf_op jit(solution)/shard_map/all_gather | solution.py:60
  539.8 4.9 collective-permute-start.16
  546.9 15.2 %collective-permute-done.16 = bf16[2,3,4,128,128]{3,4,2,0,1:T(8,128)(2,1)S(1)} collective-permute-done((bf16[2,3,4,128,128]{3,4,2,0,1:T(8,128)(2,1)S(1)}, bf16[2,3,4,128,128]{3,4,2,0,1:T(8,128)(2,1)S(1)}, u32[]{:S(2)}, u32[]{:S(2)}) %collective-permute-start.16) | collective-permute-done | bytes 786464 | tf_op jit(solution)/shard_map/ppermute | solution.py:19
  562.1 5.2 collective-permute-done.17
  588.8 29.2 %all-gather.23.cloned.1.call-done = bf16[2,6,4,128,128]{3,4,2,0,1:T(8,128)(2,1)} async-done(((bf16[2,6,2,128,128]{3,4,2,0,1:T(8,128)(2,1)}), bf16[2,6,4,128,128]{3,4,2,0,1:T(8,128)(2,1)}) %all-gather.23.cloned.1.call-update) | async-done | bytes 1572880 | tf_op jit(solution)/shard_map/all_gather | solution.py:60
  626.6 15.4 %collective-permute-done.18 = bf16[2,3,4,128,128]{3,4,2,0,1:T(8,128)(2,1)S(1)} collective-permute-done((bf16[2,3,4,128,128]{3,4,2,0,1:T(8,128)(2,1)S(1)}, bf16[2,3,4,128,128]{3,4,2,0,1:T(8,128)(2,1)S(1)}, u32[]{:S(2)}, u32[]{:S(2)}) %collective-permute-start.18) | collective-permute-done | bytes 786464 | tf_op jit(solution)/shard_map/ppermute | solution.py:19
  642.0 5.2 collective-permute-done.19
  (212 shorter events, 235.2 us)
Async XLA Ops:
  6.5 52.6 %all-gather.9.cloned.1.call-start = ((), (), s32[]{:S(2)}) async-start(), calls=%async_computation | async-start | bytes 2359296 | tf_op jit(solution)/shard_map/all_gather | solution.py:60
  7.4 29.1 %collective-permute-start.2 = (s32[3,4]{0,1:T(4,128)S(1)}, s32[3,4]{0,1:T(4,128)S(1)}, u32[]{:S(2)}, u32[]{:S(2)}) collective-permute-start(s32[3,4]{0,1:T(4,128)S(1)} %get-tuple-element.40), channel_id=1, source_target_pairs={{0,2},{2,4},{4,6},{6,8},{8,10},{10,12},{12,14},{14,16},{16,18},{18... | collective-permute-start | bytes 152 | tf_op jit(solution)/shard_map/ppermute | solution.py:19
  12.7 23.7 %collective-permute-start.3 = (s32[3,4]{0,1:T(4,128)S(1)}, s32[3,4]{0,1:T(4,128)S(1)}, u32[]{:S(2)}, u32[]{:S(2)}) collective-permute-start(s32[3,4]{0,1:T(4,128)S(1)} %get-tuple-element.41), channel_id=1, source_target_pairs={{2,0},{4,2},{6,4},{8,6},{10,8},{12,10},{14,12},{16,14},{18,16},{20... | collective-permute-start | bytes 152 | tf_op jit(solution)/shard_map/ppermute | solution.py:21
  16.8 117.1 %all-gather.11.cloned.1.call-start = ((), (), s32[]{:S(2)}) async-start(), calls=%async_computation.1 | async-start | bytes 2359296 | tf_op jit(solution)/shard_map/all_gather | solution.py:60
  24.2 45.0 %collective-permute-start.4 = (bf16[3,4,128,128]{3,2,1,0:T(8,128)(2,1)S(1)}, bf16[3,4,128,128]{3,2,1,0:T(8,128)(2,1)S(1)}, u32[]{:S(2)}, u32[]{:S(2)}) collective-permute-start(bf16[3,4,128,128]{3,2,1,0:T(8,128)(2,1)S(1)} %get-tuple-element.38), channel_id=1, source_target_pairs={{0,2},{2,4},{4,6},{6,8},{8,10},{10,12},{12,14},{14,16},{16,18},{18... | collective-permute-start | bytes 1179656 | tf_op jit(solution)/shard_map/ppermute | solution.py:19
  32.3 36.9 %collective-permute-start.5 = (bf16[3,4,128,128]{3,2,1,0:T(8,128)(2,1)S(1)}, bf16[3,4,128,128]{3,2,1,0:T(8,128)(2,1)S(1)}, u32[]{:S(2)}, u32[]{:S(2)}) collective-permute-start(bf16[3,4,128,128]{3,2,1,0:T(8,128)(2,1)S(1)} %get-tuple-element.39), channel_id=1, source_target_pairs={{2,0},{4,2},{6,4},{8,6},{10,8},{12,10},{14,12},{16,14},{18,16},{20... | collective-permute-start | bytes 1179656 | tf_op jit(solution)/shard_map/ppermute | solution.py:21
  61.8 22.6 %collective-permute-start = (bf16[2,3,4,128,128]{4,3,2,0,1:T(8,128)(2,1)}, bf16[2,3,4,128,128]{4,3,2,0,1:T(8,128)(2,1)}, u32[]{:S(2)}, u32[]{:S(2)}) collective-permute-start(bf16[2,3,4,128,128]{4,3,2,0,1:T(8,128)(2,1)} %get-tuple-element.36), channel_id=1, source_target_pairs={{0,2},{2,4},{4,6},{6,8},{8,10},{10,12},{12,14},{14,16},{16,18},{18... | collective-permute-start | bytes 2359304 | tf_op jit(solution)/shard_map/ppermute | solution.py:19
  66.7 22.8 %collective-permute-start.1 = (bf16[2,3,4,128,128]{4,3,2,0,1:T(8,128)(2,1)}, bf16[2,3,4,128,128]{4,3,2,0,1:T(8,128)(2,1)}, u32[]{:S(2)}, u32[]{:S(2)}) collective-permute-start(bf16[2,3,4,128,128]{4,3,2,0,1:T(8,128)(2,1)} %get-tuple-element.37), channel_id=1, source_target_pairs={{2,0},{4,2},{6,4},{8,6},{10,8},{12,10},{14,12},{16,14},{18,16},{20... | collective-permute-start | bytes 2359304 | tf_op jit(solution)/shard_map/ppermute | solution.py:21
  104.6 109.2 %all-gather.13.cloned.1.call-start = ((), (), s32[]{:S(2)}) async-start(), calls=%async_computation.2 | async-start | bytes 2359296 | tf_op jit(solution)/shard_map/all_gather | solution.py:60
  133.9 29.1 %copy-start.2 = (bf16[2,6,4,128,128]{3,4,2,0,1:T(8,128)(2,1)S(1)}, bf16[2,6,4,128,128]{3,4,2,0,1:T(8,128)(2,1)}, u32[]{:S(2)}) copy-start(bf16[2,6,4,128,128]{3,4,2,0,1:T(8,128)(2,1)} %all-gather.11.cloned.1.call-done) | copy-start | bytes 4718596
  135.6 22.3 %collective-permute-start.6 = (bf16[2,3,4,128,128]{3,4,2,0,1:T(8,128)(2,1)S(1)}, bf16[2,3,4,128,128]{3,4,2,0,1:T(8,128)(2,1)S(1)}, u32[]{:S(2)}, u32[]{:S(2)}) collective-permute-start(bf16[2,3,4,128,128]{3,4,2,0,1:T(8,128)(2,1)S(1)} %get-tuple-element.34), channel_id=1, source_target_pairs={{0,2},{2,4},{4,6},{6,8},{8,10},{10,12},{12,14},{14,16},{16,18},{18... | collective-permute-start | bytes 2359304 | tf_op jit(solution)/shard_map/ppermute | solution.py:19
  140.5 22.5 %collective-permute-start.7 = (bf16[2,3,4,128,128]{3,4,2,0,1:T(8,128)(2,1)S(1)}, bf16[2,3,4,128,128]{3,4,2,0,1:T(8,128)(2,1)S(1)}, u32[]{:S(2)}, u32[]{:S(2)}) collective-permute-start(bf16[2,3,4,128,128]{3,4,2,0,1:T(8,128)(2,1)S(1)} %get-tuple-element.35), channel_id=1, source_target_pairs={{2,0},{4,2},{6,4},{8,6},{10,8},{12,10},{14,12},{16,14},{18,16},{20... | collective-permute-start | bytes 2359304 | tf_op jit(solution)/shard_map/ppermute | solution.py:21
  184.6 109.2 %all-gather.15.cloned.1.call-start = ((), (), s32[]{:S(2)}) async-start(), calls=%async_computation.3 | async-start | bytes 2359296 | tf_op jit(solution)/shard_map/all_gather | solution.py:60
  213.8 29.1 %copy-start.3 = (bf16[2,6,4,128,128]{3,4,2,0,1:T(8,128)(2,1)S(1)}, bf16[2,6,4,128,128]{3,4,2,0,1:T(8,128)(2,1)}, u32[]{:S(2)}) copy-start(bf16[2,6,4,128,128]{3,4,2,0,1:T(8,128)(2,1)} %all-gather.13.cloned.1.call-done) | copy-start | bytes 4718596
  215.5 22.3 %collective-permute-start.8 = (bf16[2,3,4,128,128]{3,4,2,0,1:T(8,128)(2,1)S(1)}, bf16[2,3,4,128,128]{3,4,2,0,1:T(8,128)(2,1)S(1)}, u32[]{:S(2)}, u32[]{:S(2)}) collective-permute-start(bf16[2,3,4,128,128]{3,4,2,0,1:T(8,128)(2,1)S(1)} %get-tuple-element.30), channel_id=1, source_target_pairs={{0,2},{2,4},{4,6},{6,8},{8,10},{10,12},{12,14},{14,16},{16,18},{18... | collective-permute-start | bytes 2359304 | tf_op jit(solution)/shard_map/ppermute | solution.py:19
  220.4 22.5 %collective-permute-start.9 = (bf16[2,3,4,128,128]{3,4,2,0,1:T(8,128)(2,1)S(1)}, bf16[2,3,4,128,128]{3,4,2,0,1:T(8,128)(2,1)S(1)}, u32[]{:S(2)}, u32[]{:S(2)}) collective-permute-start(bf16[2,3,4,128,128]{3,4,2,0,1:T(8,128)(2,1)S(1)} %get-tuple-element.31), channel_id=1, source_target_pairs={{2,0},{4,2},{6,4},{8,6},{10,8},{12,10},{14,12},{16,14},{18,16},{20... | collective-permute-start | bytes 2359304 | tf_op jit(solution)/shard_map/ppermute | solution.py:21
  264.5 113.9 %all-gather.17.cloned.1.call-start = ((), (), s32[]{:S(2)}) async-start(), calls=%async_computation.4 | async-start | bytes 2359296 | tf_op jit(solution)/shard_map/all_gather | solution.py:60
  296.4 22.7 %collective-permute-start.10 = (bf16[2,3,4,128,128]{3,4,2,0,1:T(8,128)(2,1)}, bf16[2,3,4,128,128]{3,4,2,0,1:T(8,128)(2,1)}, u32[]{:S(2)}, u32[]{:S(2)}) collective-permute-start(bf16[2,3,4,128,128]{3,4,2,0,1:T(8,128)(2,1)} %get-tuple-element.26), channel_id=1, source_target_pairs={{0,2},{2,4},{4,6},{6,8},{8,10},{10,12},{12,14},{14,16},{16,18},{18... | collective-permute-start | bytes 2359304 | tf_op jit(solution)/shard_map/ppermute | solution.py:19
  301.5 22.8 %collective-permute-start.11 = (bf16[2,3,4,128,128]{3,4,2,0,1:T(8,128)(2,1)}, bf16[2,3,4,128,128]{3,4,2,0,1:T(8,128)(2,1)}, u32[]{:S(2)}, u32[]{:S(2)}) collective-permute-start(bf16[2,3,4,128,128]{3,4,2,0,1:T(8,128)(2,1)} %get-tuple-element.27), channel_id=1, source_target_pairs={{2,0},{4,2},{6,4},{8,6},{10,8},{12,10},{14,12},{16,14},{18,16},{20... | collective-permute-start | bytes 2359304 | tf_op jit(solution)/shard_map/ppermute | solution.py:21
  349.2 109.1 %all-gather.19.cloned.1.call-start = ((), (), s32[]{:S(2)}) async-start(), calls=%async_computation.5 | async-start | bytes 2359296 | tf_op jit(solution)/shard_map/all_gather | solution.py:60
  378.4 29.1 %copy-start.4 = (bf16[2,6,4,128,128]{3,4,2,0,1:T(8,128)(2,1)S(1)}, bf16[2,6,4,128,128]{3,4,2,0,1:T(8,128)(2,1)}, u32[]{:S(2)}) copy-start(bf16[2,6,4,128,128]{3,4,2,0,1:T(8,128)(2,1)} %all-gather.17.cloned.1.call-done) | copy-start | bytes 4718596
  380.1 22.3 %collective-permute-start.12 = (bf16[2,3,4,128,128]{3,4,2,0,1:T(8,128)(2,1)S(1)}, bf16[2,3,4,128,128]{3,4,2,0,1:T(8,128)(2,1)S(1)}, u32[]{:S(2)}, u32[]{:S(2)}) collective-permute-start(bf16[2,3,4,128,128]{3,4,2,0,1:T(8,128)(2,1)S(1)} %get-tuple-element.22), channel_id=1, source_target_pairs={{0,2},{2,4},{4,6},{6,8},{8,10},{10,12},{12,14},{14,16},{16,18},{18... | collective-permute-start | bytes 2359304 | tf_op jit(solution)/shard_map/ppermute | solution.py:19
  385.0 22.5 %collective-permute-start.13 = (bf16[2,3,4,128,128]{3,4,2,0,1:T(8,128)(2,1)S(1)}, bf16[2,3,4,128,128]{3,4,2,0,1:T(8,128)(2,1)S(1)}, u32[]{:S(2)}, u32[]{:S(2)}) collective-permute-start(bf16[2,3,4,128,128]{3,4,2,0,1:T(8,128)(2,1)S(1)} %get-tuple-element.23), channel_id=1, source_target_pairs={{2,0},{4,2},{6,4},{8,6},{10,8},{12,10},{14,12},{16,14},{18,16},{20... | collective-permute-start | bytes 2359304 | tf_op jit(solution)/shard_map/ppermute | solution.py:21
  429.0 109.1 %all-gather.21.cloned.1.call-start = ((), (), s32[]{:S(2)}) async-start(), calls=%async_computation.6 | async-start | bytes 2359296 | tf_op jit(solution)/shard_map/all_gather | solution.py:60
  459.9 22.3 %collective-permute-start.14 = (bf16[2,3,4,128,128]{3,4,2,0,1:T(8,128)(2,1)S(1)}, bf16[2,3,4,128,128]{3,4,2,0,1:T(8,128)(2,1)S(1)}, u32[]{:S(2)}, u32[]{:S(2)}) collective-permute-start(bf16[2,3,4,128,128]{3,4,2,0,1:T(8,128)(2,1)S(1)} %get-tuple-element.20), channel_id=1, source_target_pairs={{0,2},{2,4},{4,6},{6,8},{8,10},{10,12},{12,14},{14,16},{16,18},{18... | collective-permute-start | bytes 2359304 | tf_op jit(solution)/shard_map/ppermute | solution.py:19
  464.8 22.5 %collective-permute-start.15 = (bf16[2,3,4,128,128]{3,4,2,0,1:T(8,128)(2,1)S(1)}, bf16[2,3,4,128,128]{3,4,2,0,1:T(8,128)(2,1)S(1)}, u32[]{:S(2)}, u32[]{:S(2)}) collective-permute-start(bf16[2,3,4,128,128]{3,4,2,0,1:T(8,128)(2,1)S(1)} %get-tuple-element.21), channel_id=1, source_target_pairs={{2,0},{4,2},{6,4},{8,6},{10,8},{12,10},{14,12},{16,14},{18,16},{20... | collective-permute-start | bytes 2359304 | tf_op jit(solution)/shard_map/ppermute | solution.py:21
  508.9 109.2 %all-gather.23.cloned.1.call-start = ((), (), s32[]{:S(2)}) async-start(), calls=%async_computation.7 | async-start | bytes 2359296 | tf_op jit(solution)/shard_map/all_gather | solution.py:60
  538.1 29.1 %copy-start.6 = (bf16[2,6,4,128,128]{3,4,2,0,1:T(8,128)(2,1)S(1)}, bf16[2,6,4,128,128]{3,4,2,0,1:T(8,128)(2,1)}, u32[]{:S(2)}) copy-start(bf16[2,6,4,128,128]{3,4,2,0,1:T(8,128)(2,1)} %all-gather.21.cloned.1.call-done) | copy-start | bytes 4718596
  539.8 22.3 %collective-permute-start.16 = (bf16[2,3,4,128,128]{3,4,2,0,1:T(8,128)(2,1)S(1)}, bf16[2,3,4,128,128]{3,4,2,0,1:T(8,128)(2,1)S(1)}, u32[]{:S(2)}, u32[]{:S(2)}) collective-permute-start(bf16[2,3,4,128,128]{3,4,2,0,1:T(8,128)(2,1)S(1)} %get-tuple-element.16), channel_id=1, source_target_pairs={{0,2},{2,4},{4,6},{6,8},{8,10},{10,12},{12,14},{14,16},{16,18},{18... | collective-permute-start | bytes 2359304 | tf_op jit(solution)/shard_map/ppermute | solution.py:19
  544.7 22.5 %collective-permute-start.17 = (bf16[2,3,4,128,128]{3,4,2,0,1:T(8,128)(2,1)S(1)}, bf16[2,3,4,128,128]{3,4,2,0,1:T(8,128)(2,1)S(1)}, u32[]{:S(2)}, u32[]{:S(2)}) collective-permute-start(bf16[2,3,4,128,128]{3,4,2,0,1:T(8,128)(2,1)S(1)} %get-tuple-element.17), channel_id=1, source_target_pairs={{2,0},{4,2},{6,4},{8,6},{10,8},{12,10},{14,12},{16,14},{18,16},{20... | collective-permute-start | bytes 2359304 | tf_op jit(solution)/shard_map/ppermute | solution.py:21
  619.7 22.3 %collective-permute-start.18 = (bf16[2,3,4,128,128]{3,4,2,0,1:T(8,128)(2,1)S(1)}, bf16[2,3,4,128,128]{3,4,2,0,1:T(8,128)(2,1)S(1)}, u32[]{:S(2)}, u32[]{:S(2)}) collective-permute-start(bf16[2,3,4,128,128]{3,4,2,0,1:T(8,128)(2,1)S(1)} %get-tuple-element.12), channel_id=1, source_target_pairs={{0,2},{2,4},{4,6},{6,8},{8,10},{10,12},{12,14},{14,16},{16,18},{18... | collective-permute-start | bytes 2359304 | tf_op jit(solution)/shard_map/ppermute | solution.py:19
  624.7 22.5 %collective-permute-start.19 = (bf16[2,3,4,128,128]{3,4,2,0,1:T(8,128)(2,1)S(1)}, bf16[2,3,4,128,128]{3,4,2,0,1:T(8,128)(2,1)S(1)}, u32[]{:S(2)}, u32[]{:S(2)}) collective-permute-start(bf16[2,3,4,128,128]{3,4,2,0,1:T(8,128)(2,1)S(1)} %get-tuple-element.13), channel_id=1, source_target_pairs={{2,0},{4,2},{6,4},{8,6},{10,8},{12,10},{14,12},{16,14},{18,16},{20... | collective-permute-start | bytes 2359304 | tf_op jit(solution)/shard_map/ppermute | solution.py:21
  (22 other events, 152.3 us)
Sparse Core Ops, SparseCore 0:
  16.9 42.1 all-gather.8
  104.8 29.0 all-gather.10
  184.7 29.0 all-gather.12
  264.6 29.0 all-gather.14
  349.3 29.0 all-gather.16
  429.1 29.0 all-gather.18
  509.0 29.0 all-gather.20
  588.9 29.0 all-gather.22
where the time goes:
time: 690 us; the launch traced here: 679 us
  waiting for transfers between devices  384 us (56%)
  local copies, waits for them, and re-layouts  142 us (21%)
  starting transfers between devices  73.2 us (11%)
  other arithmetic  43.4 us (6%)
  matrix products  14.7 us (2%)
  between operations  14.6 us (2%)
  blocking collectives  7.3 us (1%)
    all_gather x8, waiting for transfers between devices, shards(): term_rows = lax.all_gather(series_term, 'col', axis=2, tiled=True)  226 us
    ppermute x10, waiting for transfers between devices, padded(): lax.ppermute(tail, axis, [(i, (i + 1) % count) for i in range(ends)])  116 us
    ppermute x10, starting transfers between devices, padded(): lax.ppermute(tail, axis, [(i, (i + 1) % count) for i in range(ends)])  52.9 us
    ppermute x10, waiting for transfers between devices, padded(): lax.ppermute(head, axis, [((i + 1) % count, i) for i in range(ends)])  41.5 us
    gather x8, local copies, waits for them, and re-layouts, shards(): picked_term = jnp.take(term_flat, flat_index, axis=1)  37.2 us
    concatenate x9, local copies, waits for them, and re-layouts, padded(): jnp.concatenate([lax.ppermute(tail, axis, [(i, (i + 1) % count) for i in...  32.9 us
    concatenate x8, local copies, waits for them, and re-layouts, shards(): jnp.concatenate([term_wide.reshape(2, -1, block_size, block_size), zero_p...  29.7 us
    ppermute x10, starting transfers between devices, padded(): lax.ppermute(head, axis, [((i + 1) % count, i) for i in range(ends)])  20.1 us
  transfers between devices with their start and end apart: 28, of which 24 were waited for; matrix products, arithmetic and copies ran while one was open for 2% of the time, Pallas kernels for 0%

commit v1 on v0

v1 whole, which is shorter than its diff:
```python
import functools

import jax
import jax.numpy as jnp
import numpy as np
from jax import lax
from jax.experimental import pallas as pl
from jax.experimental.pallas import tpu as pltpu
from jax.sharding import PartitionSpec as P

STEPS = 2
ORDERS = 4


def series_weights():
    factorial = [1]
    for n in range(1, STEPS * ORDERS + 1):
        factorial.append(factorial[-1] * n)
    once = [1.0 / factorial[n] for n in range(ORDERS + 1)]
    power = [1.0]
    for _ in range(STEPS):
        power = list(np.convolve(power, once))
    return [float(power[n] * factorial[n]) for n in range(STEPS * ORDERS + 1)]


WEIGHT = [(-1.0) ** (m // 2) * w for m, w in enumerate(series_weights())]
AXES = ("dom", "col")
ROWS = 6
SLOTS = 4
BLOCK = 128
HALF = ROWS * SLOTS // 2
OWN = ROWS * SLOTS
ZERO = 3 * OWN
TAB = 20


def flat_of(group, y, core):
    return ((group * 2 + y // 2) * 2 + core) * 2 + y % 2


def place_of(group, part, core, chain, groups):
    group = group % groups
    low = part ^ chain ^ (group % 2)
    return flat_of(group, chain * 2 + low, core)


def routes(groups):
    turn, keep, inner, outer = {}, {}, {}, {}
    left, right = {}, {}
    for group in range(groups):
        odd = group % 2
        for core in range(2):
            for y in range(4):
                here = flat_of(group, y, core)
                turn[here] = flat_of(group, (y + (1 if odd else 3)) % 4, core)
                stays = y % 2 == odd
                keep[here] = here if stays else flat_of(group, y ^ 2, core)
                inner[here] = flat_of(group, y, 1 - core)
                chain = y // 2
                part = chain ^ (y % 2) ^ odd
                ahead = (group, 1) if part == 0 else (group + 1, 0)
                behind = (group, 0) if part == 1 else (group - 1, 1)
                before = place_of(*behind, 1, chain, groups)
                after = place_of(*ahead, 0, chain, groups)
                outer[here] = after if core else before
                left[here] = inner[here] if core else before
                right[here] = after if core else inner[here]
    back = {target: source for source, target in turn.items()}
    pairs = lambda table: sorted(table.items())
    return {
        "turn": pairs(turn),
        "keep": pairs(keep),
        "turn_back": pairs(back),
        "keep_back": sorted((b, a) for a, b in keep.items()),
        "inner": pairs(inner),
        "outer": pairs(outer),
        "from_left": sorted((back[left[here]], here) for here in turn),
        "from_right": sorted((back[right[here]], here) for here in turn),
    }


def index_table(neighbours, route, group, core, chain, low, part):
    own = lax.ppermute(neighbours, AXES, route["turn"])
    left = lax.ppermute(neighbours, AXES, route["from_left"])
    right = lax.ppermute(neighbours, AXES, route["from_right"])
    left_low = jnp.where((core == 0) & (part == 1), 1 - low, low)
    right_low = jnp.where((core == 1) & (part == 0), 1 - low, low)
    turned = lambda lists, swap: jnp.where(swap == 1, jnp.roll(lists, 2, axis=1), lists)
    own, left, right = turned(own, low), turned(left, left_low), turned(right, right_low)
    first = (group * 4 + part * 2 + core - 1) * ROWS
    wide = jnp.concatenate([left, own, right], axis=0)
    lists = jnp.concatenate([own, left[3:], right[:3]], axis=0)
    where_rows = jnp.array(list(range(6, 12)) + [3, 4, 5, 12, 13, 14], jnp.int32)

    def flat(place, slot):
        side = place // ROWS
        row = place - side * ROWS
        outside = jnp.where((side == 0) == (core == 1), 0, 2)
        box = jnp.where(side == 1, 1, outside)
        return box * OWN + (slot // 2) * HALF + row * 2 + slot % 2

    place = lists - first
    inside = (place >= 0) & (place < 3 * ROWS)
    place = jnp.clip(place, 0, 3 * ROWS - 1)
    rows_of = jnp.take(wide, place, axis=0)
    matches = rows_of[:, None, :, :] == lists[:, :, None, None]
    present = jnp.any(matches, axis=-1) & inside[:, None, :]
    slot_iota = jnp.arange(SLOTS, dtype=jnp.int32)
    slot = jnp.sum(jnp.where(matches, slot_iota, 0), axis=-1)
    picked = jnp.where(present, flat(place[:, None, :], slot), ZERO)
    mine = flat(where_rows[:, None], slot_iota[None, :])
    table = jnp.concatenate([picked.reshape(-1, SLOTS * SLOTS), mine], axis=1)
    return jnp.concatenate([table.reshape(-1), chain[None]]).astype(jnp.int32)


def bracket(table, row, operator, term, inverse):
    at = lambda n: table[row * TAB + n]
    mine = [at(SLOTS * SLOTS + t) for t in range(SLOTS)]
    pick = [[at(s * SLOTS + t) for s in range(SLOTS)] for t in range(SLOTS)]
    wide = lambda ref, places: jnp.concatenate([ref[n] for n in places], axis=1)
    tall = lambda ref: jnp.concatenate([wide(ref, places) for places in pick], axis=0)
    left = jnp.dot(wide(operator, mine), tall(term), preferred_element_type=jnp.float32)
    right = jnp.dot(wide(term, mine), tall(operator), preferred_element_type=jnp.float32)
    fresh = ((left - right) * inverse).astype(jnp.bfloat16)
    return mine, [fresh[:, s * BLOCK : (s + 1) * BLOCK] for s in range(SLOTS)]


def two_orders(order, last, table, operator, own, inner, outer, *rest):
    if last:
        even_sum, odd_sum, kept, moved, term, first = rest
    else:
        first_out, second_out, term, first = rest
    zero = jnp.zeros((BLOCK, BLOCK), jnp.bfloat16)
    term[0:OWN] = inner[...]
    term[OWN : 2 * OWN] = own[...]
    term[2 * OWN : 3 * OWN] = outer[...]
    term[ZERO] = zero
    first[ZERO] = zero

    def first_row(row, carry):
        mine, blocks = bracket(table, row, operator, term, 1.0 / order)
        for n, block in zip(mine, blocks):
            first[n] = block
        return carry

    lax.fori_loop(0, 2 * ROWS, first_row, 0)

    if not last:
        first_out[...] = first[OWN : 2 * OWN]

    def second_row(row, carry):
        mine, blocks = bracket(table, row, operator, first, 1.0 / (order + 1))
        for n, block in zip(mine, blocks):
            if last:
                term[n] = block
            else:
                second_out[n - OWN] = block
        return carry

    lax.fori_loop(0, ROWS, second_row, 0)

    if last:
        chain = table[2 * ROWS * TAB]
        sign = jnp.where(chain == 0, -1.0, 1.0).astype(jnp.float32)

        def join(n, carry):
            for half, out in ((0, kept), (1, moved)):
                at = half * HALF + n
                even = even_sum[at] + WEIGHT[order + 1] * term[OWN + at].astype(jnp.float32)
                odd = odd_sum[at] + WEIGHT[order] * first[OWN + at].astype(jnp.float32)
                out[chain * HALF + n] = even.astype(jnp.bfloat16)
                out[(1 - chain) * HALF + n] = (sign * odd).astype(jnp.bfloat16)
            return carry

        lax.fori_loop(0, HALF, join, 0)


def run_orders(order, last, table, operator, own, inner, outer, sums=()):
    blocks = jax.ShapeDtypeStruct((OWN, BLOCK, BLOCK), jnp.bfloat16)
    vmem = pl.BlockSpec(memory_space=pltpu.VMEM)
    return pl.pallas_call(
        functools.partial(two_orders, order, last),
        out_shape=(blocks, blocks),
        in_specs=[pl.BlockSpec(memory_space=pltpu.SMEM)] + [vmem] * (4 + len(sums)),
        out_specs=(vmem, vmem),
        scratch_shapes=[pltpu.VMEM((ZERO + 1, BLOCK, BLOCK), jnp.bfloat16)] * 2,
        compiler_params=pltpu.CompilerParams(vmem_limit_bytes=32 * 1024 * 1024),
        cost_estimate=pl.CostEstimate(
            flops=18 * 2 * 2 * 128 * 512 * 512, bytes_accessed=6 * 2**20, transcendentals=0
        ),
        name="two_orders",
    )(table, operator, own, inner, outer, *sums)


def shards(groups, density, hamiltonian, neighbours):
    domain, low = lax.axis_index("dom"), lax.axis_index("col")
    route = routes(groups)
    group, chain, core = domain // 4, (domain // 2) % 2, domain % 2
    odd = group % 2
    part = chain ^ low ^ odd
    move = functools.partial(lax.ppermute, axis_name=AXES)

    own_h = hamiltonian.reshape(HALF, BLOCK, BLOCK)
    turn_part = chain ^ low ^ 1 ^ odd
    turn_x = lax.dynamic_index_in_dim(density, turn_part, 0, False).reshape(HALF, BLOCK, BLOCK)
    keep_x = lax.dynamic_index_in_dim(density, 1 - turn_part, 0, False).reshape(HALF, BLOCK, BLOCK)
    turn_h = move(own_h, perm=route["turn"])
    keep_h = move(own_h, perm=route["keep"])
    turn_x = move(turn_x, perm=route["turn"])
    keep_x = move(keep_x, perm=route["keep"])
    table = index_table(neighbours, route, group, core, chain, low, part)
    operator = jnp.concatenate([keep_h, turn_h], axis=0)
    operator = jnp.concatenate(
        [
            move(operator, perm=route["inner"]),
            operator,
            move(operator, perm=route["outer"]),
            jnp.zeros((1, BLOCK, BLOCK), jnp.bfloat16),
        ],
        axis=0,
    )
    term = jnp.concatenate([keep_x, turn_x], axis=0)
    sums = [term.astype(jnp.float32) * WEIGHT[0], jnp.zeros((), jnp.float32)]
    count = STEPS * ORDERS
    for order in range(1, count, 2):
        outer = move(term, perm=route["outer"])
        inner = move(term, perm=route["inner"])
        last = order + 1 == count
        first, term = run_orders(
            order, last, table, operator, term, inner, outer, tuple(sums) if last else ()
        )
        if not last:
            sums[1] = sums[1] + WEIGHT[order] * first.astype(jnp.float32)
            sums[0] = sums[0] + WEIGHT[order + 1] * term.astype(jnp.float32)
    kept = move(first, perm=route["keep_back"])
    moved = move(term, perm=route["turn_back"])
    total = kept.astype(jnp.float32) + moved.astype(jnp.float32)
    return total.reshape(density.shape)


def solution(mesh):
    placed = (P(None, "dom", "col", None, None), P("dom", "col", None, None), P("dom", None))
    return jax.shard_map(
        functools.partial(shards, mesh.shape["dom"] // 4),
        mesh=mesh,
        in_specs=placed,
        out_specs=P(None, "dom", "col", None, None),
        check_vma=False,
    )
```

time: 690 us -> 149 us (0.22)
  the two profiles are of different devices: /device:TPU:129 before, /device:TPU:24 now
where the time goes in v1:
time: 149 us; the launch traced here: 147 us
  waiting for transfers between devices  70.2 us (47%)
  starting transfers between devices  39.6 us (27%)
  Pallas kernels  26.8 us (18%)
  local copies, waits for them, and re-layouts  6.73 us (5%)
  other arithmetic  3.66 us (2%)
    ppermute x4, waiting for transfers between devices, shards(): outer = move(term, perm=route['outer'])  39.6 us
    pallas_call x4, Pallas kernels, run_orders(): pl.pallas_call(functools.partial(two_orders, order, last), out_shape=(blo...  26.8 us
    ppermute x4, starting transfers between devices, shards(): outer = move(term, perm=route['outer'])  16 us
    ppermute x1, waiting for transfers between devices, shards(): kept = move(first, perm=route['keep_back'])  13 us
    ppermute x1, waiting for transfers between devices, shards(): keep_h = move(own_h, perm=route['keep'])  11.1 us
    ppermute x1, starting transfers between devices, shards(): keep_h = move(own_h, perm=route['keep'])  9.22 us
    ppermute x1, starting transfers between devices, shards(): move(operator, perm=route['outer'])  5.55 us
    ppermute x1, waiting for transfers between devices, shards(): turn_x = move(turn_x, perm=route['turn'])  5.35 us
  transfers between devices with their start and end apart: 19, of which 8 were waited for; matrix products, arithmetic and copies ran while one was open for 6% of the time, Pallas kernels for 0%

profile of v1, /device:TPU:24, one launch (start us, length us, event | category | flops | bytes accessed | tf_op | source)
XLA Modules:
  0.0 147.4 jit_solution(678574508239772990)
XLA Ops:
  0.0 0.7 collective-permute-start
  0.7 2.4 %collective-permute-start.1 = (s32[6,4]{0,1:T(4,128)}, s32[6,4]{0,1:T(4,128)S(1)}, u32[]{:S(2)}, u32[]{:S(2)}) collective-permute-start(s32[6,4]{0,1:T(4,128)} %param.6), channel_id=1, source_target_pairs={{0,7},{1,2},{2,4},{3,1},{4,3},{5,6},{6,9},{7,12},{8,11},{9,14},{10... | collective-permute-start | bytes 296 | tf_op jit(solution)/shard_map/ppermute | solution.py:84
  3.1 1.3 collective-permute-start.4
  4.4 9.2 %collective-permute-start.3 = (bf16[12,128,128]{2,1,0:T(8,128)(2,1)}, bf16[12,128,128]{2,1,0:T(8,128)(2,1)S(1)}, u32[]{:S(2)}, u32[]{:S(2)}) collective-permute-start(bf16[12,128,128]{2,1,0:T(8,128)(2,1)} %bitcast.31), channel_id=1, source_target_pairs={{0,0},{1,5},{2,2},{3,7},{4,4},{5,1},{6,6},{7,3},{8,12},{9,9},{10,1... | collective-permute-start | bytes 1179656 | tf_op jit(solution)/shard_map/ppermute | solution.py:208
  13.7 0.7 fusion.14
  14.4 1.2 constant_dynamic-slice_fusion
  15.7 1.9 %collective-permute-start.7 = (bf16[12,128,128]{2,1,0:T(8,128)(2,1)S(1)}, bf16[12,128,128]{2,1,0:T(8,128)(2,1)S(1)}, u32[]{:S(2)}, u32[]{:S(2)}) collective-permute-start(bf16[12,128,128]{2,1,0:T(8,128)(2,1)S(1)} %bitcast.21), channel_id=1, source_target_pairs={{0,0},{1,5},{2,2},{3,7},{4,4},{5,1},{6,6},{7,3},{8,12},{9,9},{10,1... | collective-permute-start | bytes 1179656 | tf_op jit(solution)/shard_map/ppermute | solution.py:210
  18.5 0.6 gather_fusion
  19.4 11.1 %collective-permute-done.3 = bf16[12,128,128]{2,1,0:T(8,128)(2,1)S(1)} collective-permute-done((bf16[12,128,128]{2,1,0:T(8,128)(2,1)}, bf16[12,128,128]{2,1,0:T(8,128)(2,1)S(1)}, u32[]{:S(2)}, u32[]{:S(2)}) %collective-permute-start.3) | collective-permute-done | bytes 393248 | tf_op jit(solution)/shard_map/ppermute | solution.py:208
  30.5 0.8 constant_dynamic-update-slice_fusion.1
  31.2 0.8 constant_dynamic-update-slice_fusion
  32.1 5.6 %collective-permute-start.6 = (bf16[24,128,128]{2,1,0:T(8,128)(2,1)}, bf16[24,128,128]{2,1,0:T(8,128)(2,1)}, u32[]{:S(2)}, u32[]{:S(2)}) collective-permute-start(bf16[24,128,128]{2,1,0:T(8,128)(2,1)} %constant_dynamic-update-slice_fusion), channel_id=1, source_target_pairs={{0,250},{1,2},{2,1},{3,9},{4,7},{5,255},{6,12},{7,4},{8,11},{9,3},... | collective-permute-start | bytes 2359304 | tf_op jit(solution)/shard_map/ppermute | solution.py:217
  37.7 1.2 collective-permute-done.7
  38.9 5.4 %collective-permute-done.8 = bf16[12,128,128]{2,1,0:T(8,128)(2,1)S(1)} collective-permute-done((bf16[12,128,128]{2,1,0:T(8,128)(2,1)S(1)}, bf16[12,128,128]{2,1,0:T(8,128)(2,1)S(1)}, u32[]{:S(2)}, u32[]{:S(2)}) %collective-permute-start.8) | collective-permute-done | bytes 393248 | tf_op jit(solution)/shard_map/ppermute | solution.py:209
  44.3 4.0 %collective-permute-start.10 = (bf16[24,128,128]{2,1,0:T(8,128)(2,1)S(1)}, bf16[24,128,128]{2,1,0:T(8,128)(2,1)S(1)}, u32[]{:S(2)}, u32[]{:S(2)}) collective-permute-start(bf16[24,128,128]{2,1,0:T(8,128)(2,1)S(1)} %constant_dynamic-update-slice_fusion.7.own), channel_id=1, source_target_pairs={{0,250},{1,2},{2,1},{3,9},{4,7},{5,255},{6,12},{7,4},{8,11},{9,3},... | collective-permute-start | bytes 2359304 | tf_op jit(solution)/shard_map/ppermute | solution.py:226
  48.5 1.2 constant_dynamic-update-slice_fusion.6
  49.9 1.3 constant_dynamic-update-slice_fusion.3
  51.1 8.0 %collective-permute-done.10.outer = bf16[24,128,128]{2,1,0:T(8,128)(2,1)S(1)} collective-permute-done((bf16[24,128,128]{2,1,0:T(8,128)(2,1)S(1)}, bf16[24,128,128]{2,1,0:T(8,128)(2,1)S(1)}, u32[]{:S(2)}, u32[]{:S(2)}) %collective-permute-start.10) | collective-permute-done | bytes 786464 | tf_op jit(solution)/shard_map/ppermute | solution.py:226
  59.1 6.6 %two_orders.4 = (bf16[24,128,128]{2,1,0:T(8,128)(2,1)S(1)}, bf16[24,128,128]{2,1,0:T(8,128)(2,1)S(1)}) custom-call(s32[241]{0:T(256)S(1)} %pad_add_fusion.3.table, bf16[73,128,128]{2,1,0:T(8,128)(2,1)S(1)} %constant_dynamic-update-slice_fusion.2.operator, bf16[24,128,128]{2,1,0:T(8,128)(2,1)S(1)} %constant_dynamic-update-slice_fusion.7.own, ...), custom_call_target="tpu_custom_call" | custom-call | flops 2415919104 | bytes 6291456 | tf_op jit(solution)/shard_map/two_orders/pallas_call | solution.py:181
  65.7 4.0 %collective-permute-start.12 = (bf16[24,128,128]{2,1,0:T(8,128)(2,1)S(1)}, bf16[24,128,128]{2,1,0:T(8,128)(2,1)S(1)}, u32[]{:S(2)}, u32[]{:S(2)}) collective-permute-start(bf16[24,128,128]{2,1,0:T(8,128)(2,1)S(1)} %get-tuple-element.13.own), channel_id=1, source_target_pairs={{0,250},{1,2},{2,1},{3,9},{4,7},{5,255},{6,12},{7,4},{8,11},{9,3},... | collective-permute-start | bytes 2359304 | tf_op jit(solution)/shard_map/ppermute | solution.py:226
  69.7 10.9 %collective-permute-done.12.outer = bf16[24,128,128]{2,1,0:T(8,128)(2,1)S(1)} collective-permute-done((bf16[24,128,128]{2,1,0:T(8,128)(2,1)S(1)}, bf16[24,128,128]{2,1,0:T(8,128)(2,1)S(1)}, u32[]{:S(2)}, u32[]{:S(2)}) %collective-permute-start.12) | collective-permute-done | bytes 786464 | tf_op jit(solution)/shard_map/ppermute | solution.py:226
  80.5 6.6 %two_orders.5 = (bf16[24,128,128]{2,1,0:T(8,128)(2,1)S(1)}, bf16[24,128,128]{2,1,0:T(8,128)(2,1)S(1)}) custom-call(s32[241]{0:T(256)S(1)} %pad_add_fusion.3.table, bf16[73,128,128]{2,1,0:T(8,128)(2,1)S(1)} %constant_dynamic-update-slice_fusion.2.operator, bf16[24,128,128]{2,1,0:T(8,128)(2,1)S(1)} %get-tuple-element.13.own, ...), custom_call_target="tpu_custom_call" | custom-call | flops 2415919104 | bytes 6291456 | tf_op jit(solution)/shard_map/two_orders/pallas_call | solution.py:181
  87.1 4.0 %collective-permute-start.14 = (bf16[24,128,128]{2,1,0:T(8,128)(2,1)S(1)}, bf16[24,128,128]{2,1,0:T(8,128)(2,1)S(1)}, u32[]{:S(2)}, u32[]{:S(2)}) collective-permute-start(bf16[24,128,128]{2,1,0:T(8,128)(2,1)S(1)} %get-tuple-element.14.own), channel_id=1, source_target_pairs={{0,250},{1,2},{2,1},{3,9},{4,7},{5,255},{6,12},{7,4},{8,11},{9,3},... | collective-permute-start | bytes 2359304 | tf_op jit(solution)/shard_map/ppermute | solution.py:226
  91.1 10.9 %collective-permute-done.14.outer = bf16[24,128,128]{2,1,0:T(8,128)(2,1)S(1)} collective-permute-done((bf16[24,128,128]{2,1,0:T(8,128)(2,1)S(1)}, bf16[24,128,128]{2,1,0:T(8,128)(2,1)S(1)}, u32[]{:S(2)}, u32[]{:S(2)}) %collective-permute-start.14) | collective-permute-done | bytes 786464 | tf_op jit(solution)/shard_map/ppermute | solution.py:226
  102.0 6.6 %two_orders.6 = (bf16[24,128,128]{2,1,0:T(8,128)(2,1)S(1)}, bf16[24,128,128]{2,1,0:T(8,128)(2,1)S(1)}) custom-call(s32[241]{0:T(256)S(1)} %pad_add_fusion.3.table, bf16[73,128,128]{2,1,0:T(8,128)(2,1)S(1)} %constant_dynamic-update-slice_fusion.2.operator, bf16[24,128,128]{2,1,0:T(8,128)(2,1)S(1)} %get-tuple-element.14.own, ...), custom_call_target="tpu_custom_call" | custom-call | flops 2415919104 | bytes 6291456 | tf_op jit(solution)/shard_map/two_orders/pallas_call | solution.py:181
  108.6 4.1 %collective-permute-start.16 = (bf16[24,128,128]{2,1,0:T(8,128)(2,1)S(1)}, bf16[24,128,128]{2,1,0:T(8,128)(2,1)S(1)}, u32[]{:S(2)}, u32[]{:S(2)}) collective-permute-start(bf16[24,128,128]{2,1,0:T(8,128)(2,1)S(1)} %get-tuple-element.15.own), channel_id=1, source_target_pairs={{0,250},{1,2},{2,1},{3,9},{4,7},{5,255},{6,12},{7,4},{8,11},{9,3},... | collective-permute-start | bytes 2359304 | tf_op jit(solution)/shard_map/ppermute | solution.py:226
  113.2 0.5 multiply_add_fusion.1.rest_0_
  113.7 9.9 %collective-permute-done.16.outer = bf16[24,128,128]{2,1,0:T(8,128)(2,1)S(1)} collective-permute-done((bf16[24,128,128]{2,1,0:T(8,128)(2,1)S(1)}, bf16[24,128,128]{2,1,0:T(8,128)(2,1)S(1)}, u32[]{:S(2)}, u32[]{:S(2)}) %collective-permute-start.16) | collective-permute-done | bytes 786464 | tf_op jit(solution)/shard_map/ppermute | solution.py:226
  123.6 7.0 %two_orders.7 = (bf16[24,128,128]{2,1,0:T(8,128)(2,1)S(1)}, bf16[24,128,128]{2,1,0:T(8,128)(2,1)S(1)}) custom-call(s32[241]{0:T(256)S(1)} %pad_add_fusion.3.table, bf16[73,128,128]{2,1,0:T(8,128)(2,1)S(1)} %constant_dynamic-update-slice_fusion.2.operator, bf16[24,128,128]{2,1,0:T(8,128)(2,1)S(1)} %get-tuple-element.15.own, ...), custom_call_target="tpu_custom_call" | custom-call | flops 2415919104 | bytes 6291456 | tf_op jit(solution)/shard_map/two_orders/pallas_call | solution.py:181
  130.6 1.9 %collective-permute-start.17 = (bf16[24,128,128]{2,1,0:T(8,128)(2,1)S(1)}, bf16[24,128,128]{2,1,0:T(8,128)(2,1)S(1)}, u32[]{:S(2)}, u32[]{:S(2)}) collective-permute-start(bf16[24,128,128]{2,1,0:T(8,128)(2,1)S(1)} %get-tuple-element.19), channel_id=1, source_target_pairs={{0,0},{1,5},{2,2},{3,7},{4,4},{5,1},{6,6},{7,3},{8,12},{9,9},{10,1... | collective-permute-start | bytes 2359304 | tf_op jit(solution)/shard_map/ppermute | solution.py:235
  133.0 13.0 %collective-permute-done.17 = bf16[24,128,128]{2,1,0:T(8,128)(2,1)S(1)} collective-permute-done((bf16[24,128,128]{2,1,0:T(8,128)(2,1)S(1)}, bf16[24,128,128]{2,1,0:T(8,128)(2,1)S(1)}, u32[]{:S(2)}, u32[]{:S(2)}) %collective-permute-start.17) | collective-permute-done | bytes 786464 | tf_op jit(solution)/shard_map/ppermute | solution.py:235
  146.0 1.4 convert_add_fusion
  (60 shorter events, 2.6 us)
Async XLA Ops:
  0.0 15.6 %copy-start = (s32[12]{0:T(128)S(1)}, s32[12]{0:T(128)}, u32[]{:S(2)}) copy-start(s32[12]{0:T(128)} %constant.179) | copy-start | bytes 148
  0.0 17.9 %collective-permute-start = (s32[6,4]{0,1:T(4,128)}, s32[6,4]{0,1:T(4,128)S(1)}, u32[]{:S(2)}, u32[]{:S(2)}) collective-permute-start(s32[6,4]{0,1:T(4,128)} %param.6), channel_id=1, source_target_pairs={{0,5},{1,0},{2,7},{3,2},{4,1},{5,4},{6,3},{7,6},{8,9},{9,12},{10,1... | collective-permute-start | bytes 296 | tf_op jit(solution)/shard_map/ppermute | solution.py:83
  0.7 14.9 %collective-permute-start.2 = (s32[6,4]{0,1:T(4,128)}, s32[6,4]{0,1:T(4,128)S(1)}, u32[]{:S(2)}, u32[]{:S(2)}) collective-permute-start(s32[6,4]{0,1:T(4,128)} %param.6), channel_id=1, source_target_pairs={{0,255},{1,250},{2,5},{3,0},{4,2},{5,7},{6,1},{7,4},{8,3},{9,6},{1... | collective-permute-start | bytes 296 | tf_op jit(solution)/shard_map/ppermute | solution.py:85
  0.7 16.9 %collective-permute-start.1 = (s32[6,4]{0,1:T(4,128)}, s32[6,4]{0,1:T(4,128)S(1)}, u32[]{:S(2)}, u32[]{:S(2)}) collective-permute-start(s32[6,4]{0,1:T(4,128)} %param.6), channel_id=1, source_target_pairs={{0,7},{1,2},{2,4},{3,1},{4,3},{5,6},{6,9},{7,12},{8,11},{9,14},{10... | collective-permute-start | bytes 296 | tf_op jit(solution)/shard_map/ppermute | solution.py:84
  3.1 28.1 %collective-permute-start.4 = (bf16[12,128,128]{2,1,0:T(8,128)(2,1)}, bf16[12,128,128]{2,1,0:T(8,128)(2,1)S(1)}, u32[]{:S(2)}, u32[]{:S(2)}) collective-permute-start(bf16[12,128,128]{2,1,0:T(8,128)(2,1)} %bitcast.30), channel_id=1, source_target_pairs={{0,5},{1,0},{2,7},{3,2},{4,1},{5,4},{6,3},{7,6},{8,9},{9,12},{10,1... | collective-permute-start | bytes 1179656 | tf_op jit(solution)/shard_map/ppermute | solution.py:207
  4.4 26.1 %collective-permute-start.3 = (bf16[12,128,128]{2,1,0:T(8,128)(2,1)}, bf16[12,128,128]{2,1,0:T(8,128)(2,1)S(1)}, u32[]{:S(2)}, u32[]{:S(2)}) collective-permute-start(bf16[12,128,128]{2,1,0:T(8,128)(2,1)} %bitcast.31), channel_id=1, source_target_pairs={{0,0},{1,5},{2,2},{3,7},{4,4},{5,1},{6,6},{7,3},{8,12},{9,9},{10,1... | collective-permute-start | bytes 1179656 | tf_op jit(solution)/shard_map/ppermute | solution.py:208
  15.7 23.2 %collective-permute-start.7 = (bf16[12,128,128]{2,1,0:T(8,128)(2,1)S(1)}, bf16[12,128,128]{2,1,0:T(8,128)(2,1)S(1)}, u32[]{:S(2)}, u32[]{:S(2)}) collective-permute-start(bf16[12,128,128]{2,1,0:T(8,128)(2,1)S(1)} %bitcast.21), channel_id=1, source_target_pairs={{0,0},{1,5},{2,2},{3,7},{4,4},{5,1},{6,6},{7,3},{8,12},{9,9},{10,1... | collective-permute-start | bytes 1179656 | tf_op jit(solution)/shard_map/ppermute | solution.py:210
  17.7 26.6 %collective-permute-start.8 = (bf16[12,128,128]{2,1,0:T(8,128)(2,1)S(1)}, bf16[12,128,128]{2,1,0:T(8,128)(2,1)S(1)}, u32[]{:S(2)}, u32[]{:S(2)}) collective-permute-start(bf16[12,128,128]{2,1,0:T(8,128)(2,1)S(1)} %bitcast.20), channel_id=1, source_target_pairs={{0,5},{1,0},{2,7},{3,2},{4,1},{5,4},{6,3},{7,6},{8,9},{9,12},{10,1... | collective-permute-start | bytes 1179656 | tf_op jit(solution)/shard_map/ppermute | solution.py:209
  32.0 16.5 %collective-permute-start.5 = (bf16[24,128,128]{2,1,0:T(8,128)(2,1)}, bf16[24,128,128]{2,1,0:T(8,128)(2,1)}, u32[]{:S(2)}, u32[]{:S(2)}) collective-permute-start(bf16[24,128,128]{2,1,0:T(8,128)(2,1)} %constant_dynamic-update-slice_fusion), channel_id=1, source_target_pairs={{0,2},{1,3},{2,0},{3,1},{4,6},{5,7},{6,4},{7,5},{8,10},{9,11},{10,... | collective-permute-start | bytes 2359304 | tf_op jit(solution)/shard_map/ppermute | solution.py:215
  32.1 17.7 %collective-permute-start.6 = (bf16[24,128,128]{2,1,0:T(8,128)(2,1)}, bf16[24,128,128]{2,1,0:T(8,128)(2,1)}, u32[]{:S(2)}, u32[]{:S(2)}) collective-permute-start(bf16[24,128,128]{2,1,0:T(8,128)(2,1)} %constant_dynamic-update-slice_fusion), channel_id=1, source_target_pairs={{0,250},{1,2},{2,1},{3,9},{4,7},{5,255},{6,12},{7,4},{8,11},{9,3},... | collective-permute-start | bytes 2359304 | tf_op jit(solution)/shard_map/ppermute | solution.py:217
  44.3 14.8 %collective-permute-start.10 = (bf16[24,128,128]{2,1,0:T(8,128)(2,1)S(1)}, bf16[24,128,128]{2,1,0:T(8,128)(2,1)S(1)}, u32[]{:S(2)}, u32[]{:S(2)}) collective-permute-start(bf16[24,128,128]{2,1,0:T(8,128)(2,1)S(1)} %constant_dynamic-update-slice_fusion.7.own), channel_id=1, source_target_pairs={{0,250},{1,2},{2,1},{3,9},{4,7},{5,255},{6,12},{7,4},{8,11},{9,3},... | collective-permute-start | bytes 2359304 | tf_op jit(solution)/shard_map/ppermute | solution.py:226
  48.2 10.9 %collective-permute-start.9 = (bf16[24,128,128]{2,1,0:T(8,128)(2,1)S(1)}, bf16[24,128,128]{2,1,0:T(8,128)(2,1)S(1)}, u32[]{:S(2)}, u32[]{:S(2)}) collective-permute-start(bf16[24,128,128]{2,1,0:T(8,128)(2,1)S(1)} %constant_dynamic-update-slice_fusion.7.own), channel_id=1, source_target_pairs={{0,2},{1,3},{2,0},{3,1},{4,6},{5,7},{6,4},{7,5},{8,10},{9,11},{10,... | collective-permute-start | bytes 2359304 | tf_op jit(solution)/shard_map/ppermute | solution.py:227
  65.7 14.8 %collective-permute-start.12 = (bf16[24,128,128]{2,1,0:T(8,128)(2,1)S(1)}, bf16[24,128,128]{2,1,0:T(8,128)(2,1)S(1)}, u32[]{:S(2)}, u32[]{:S(2)}) collective-permute-start(bf16[24,128,128]{2,1,0:T(8,128)(2,1)S(1)} %get-tuple-element.13.own), channel_id=1, source_target_pairs={{0,250},{1,2},{2,1},{3,9},{4,7},{5,255},{6,12},{7,4},{8,11},{9,3},... | collective-permute-start | bytes 2359304 | tf_op jit(solution)/shard_map/ppermute | solution.py:226
  69.7 10.9 %collective-permute-start.11 = (bf16[24,128,128]{2,1,0:T(8,128)(2,1)S(1)}, bf16[24,128,128]{2,1,0:T(8,128)(2,1)S(1)}, u32[]{:S(2)}, u32[]{:S(2)}) collective-permute-start(bf16[24,128,128]{2,1,0:T(8,128)(2,1)S(1)} %get-tuple-element.13.own), channel_id=1, source_target_pairs={{0,2},{1,3},{2,0},{3,1},{4,6},{5,7},{6,4},{7,5},{8,10},{9,11},{10,... | collective-permute-start | bytes 2359304 | tf_op jit(solution)/shard_map/ppermute | solution.py:227
  87.1 14.8 %collective-permute-start.14 = (bf16[24,128,128]{2,1,0:T(8,128)(2,1)S(1)}, bf16[24,128,128]{2,1,0:T(8,128)(2,1)S(1)}, u32[]{:S(2)}, u32[]{:S(2)}) collective-permute-start(bf16[24,128,128]{2,1,0:T(8,128)(2,1)S(1)} %get-tuple-element.14.own), channel_id=1, source_target_pairs={{0,250},{1,2},{2,1},{3,9},{4,7},{5,255},{6,12},{7,4},{8,11},{9,3},... | collective-permute-start | bytes 2359304 | tf_op jit(solution)/shard_map/ppermute | solution.py:226
  91.1 10.9 %collective-permute-start.13 = (bf16[24,128,128]{2,1,0:T(8,128)(2,1)S(1)}, bf16[24,128,128]{2,1,0:T(8,128)(2,1)S(1)}, u32[]{:S(2)}, u32[]{:S(2)}) collective-permute-start(bf16[24,128,128]{2,1,0:T(8,128)(2,1)S(1)} %get-tuple-element.14.own), channel_id=1, source_target_pairs={{0,2},{1,3},{2,0},{3,1},{4,6},{5,7},{6,4},{7,5},{8,10},{9,11},{10,... | collective-permute-start | bytes 2359304 | tf_op jit(solution)/shard_map/ppermute | solution.py:227
  108.6 15.0 %collective-permute-start.16 = (bf16[24,128,128]{2,1,0:T(8,128)(2,1)S(1)}, bf16[24,128,128]{2,1,0:T(8,128)(2,1)S(1)}, u32[]{:S(2)}, u32[]{:S(2)}) collective-permute-start(bf16[24,128,128]{2,1,0:T(8,128)(2,1)S(1)} %get-tuple-element.15.own), channel_id=1, source_target_pairs={{0,250},{1,2},{2,1},{3,9},{4,7},{5,255},{6,12},{7,4},{8,11},{9,3},... | collective-permute-start | bytes 2359304 | tf_op jit(solution)/shard_map/ppermute | solution.py:226
  112.7 10.9 %collective-permute-start.15 = (bf16[24,128,128]{2,1,0:T(8,128)(2,1)S(1)}, bf16[24,128,128]{2,1,0:T(8,128)(2,1)S(1)}, u32[]{:S(2)}, u32[]{:S(2)}) collective-permute-start(bf16[24,128,128]{2,1,0:T(8,128)(2,1)S(1)} %get-tuple-element.15.own), channel_id=1, source_target_pairs={{0,2},{1,3},{2,0},{3,1},{4,6},{5,7},{6,4},{7,5},{8,10},{9,11},{10,... | collective-permute-start | bytes 2359304 | tf_op jit(solution)/shard_map/ppermute | solution.py:227
  130.6 15.4 %collective-permute-start.17 = (bf16[24,128,128]{2,1,0:T(8,128)(2,1)S(1)}, bf16[24,128,128]{2,1,0:T(8,128)(2,1)S(1)}, u32[]{:S(2)}, u32[]{:S(2)}) collective-permute-start(bf16[24,128,128]{2,1,0:T(8,128)(2,1)S(1)} %get-tuple-element.19), channel_id=1, source_target_pairs={{0,0},{1,5},{2,2},{3,7},{4,4},{5,1},{6,6},{7,3},{8,12},{9,9},{10,1... | collective-permute-start | bytes 2359304 | tf_op jit(solution)/shard_map/ppermute | solution.py:235
  132.5 13.5 %collective-permute-start.18 = (bf16[24,128,128]{2,1,0:T(8,128)(2,1)S(1)}, bf16[24,128,128]{2,1,0:T(8,128)(2,1)S(1)}, u32[]{:S(2)}, u32[]{:S(2)}) collective-permute-start(bf16[24,128,128]{2,1,0:T(8,128)(2,1)S(1)} %get-tuple-element.20), channel_id=1, source_target_pairs={{0,1},{1,4},{2,3},{3,6},{4,5},{5,0},{6,7},{7,2},{8,13},{9,8},{10,1... | collective-permute-start | bytes 2359304 | tf_op jit(solution)/shard_map/ppermute | solution.py:236

commit v2 on v1

v2 whole, which is shorter than its diff:
```python
import functools

import jax
import jax.numpy as jnp
import numpy as np
from jax import lax
from jax.experimental import pallas as pl
from jax.experimental.pallas import tpu as pltpu
from jax.sharding import PartitionSpec as P

STEPS = 2
ORDERS = 4


def series_weights():
    factorial = [1]
    for n in range(1, STEPS * ORDERS + 1):
        factorial.append(factorial[-1] * n)
    once = [1.0 / factorial[n] for n in range(ORDERS + 1)]
    power = [1.0]
    for _ in range(STEPS):
        power = list(np.convolve(power, once))
    return [float(power[n] * factorial[n]) for n in range(STEPS * ORDERS + 1)]


WEIGHT = [(-1.0) ** (m // 2) * w for m, w in enumerate(series_weights())]
AXES = ("dom", "col")
ROWS = 6
SLOTS = 4
BLOCK = 128
HALF = ROWS * SLOTS // 2
OWN = ROWS * SLOTS
NEAR = 12
FAR = (0, 3, 5)
BOX = NEAR + 6
ZERO = 2 * BOX + OWN
TAB = 20
UNROLL = 6


def flat_of(group, y, core):
    return ((group * 2 + y // 2) * 2 + core) * 2 + y % 2


def place_of(group, part, core, chain, groups):
    group = group % groups
    low = part ^ chain ^ (group % 2)
    return flat_of(group, chain * 2 + low, core)


def routes(groups):
    turn, keep, relay, inner, outer = {}, {}, {}, {}, {}
    for group in range(groups):
        odd = group % 2
        for core in range(2):
            for y in range(4):
                here = flat_of(group, y, core)
                turn[here] = flat_of(group, (y + (1 if odd else 3)) % 4, core)
                relay[here] = flat_of(group, (y + (3 if odd else 1)) % 4, core)
                stays = y % 2 == odd
                keep[here] = here if stays else flat_of(group, y ^ 2, core)
                inner[here] = flat_of(group, y, 1 - core)
                chain = y // 2
                part = chain ^ (y % 2) ^ odd
                ahead = (group, 1) if part == 0 else (group + 1, 0)
                behind = (group, 0) if part == 1 else (group - 1, 1)
                before = place_of(*behind, 1, chain, groups)
                after = place_of(*ahead, 0, chain, groups)
                outer[here] = after if core else before
    back = {target: source for source, target in turn.items()}
    pairs = lambda table: sorted(table.items())
    return {
        "turn": pairs(turn),
        "keep": pairs(keep),
        "relay": pairs(relay),
        "turn_back": pairs(back),
        "keep_back": sorted((b, a) for a, b in keep.items()),
        "inner": pairs(inner),
        "outer": pairs(outer),
    }


def own_flat(row, slot):
    return (slot // 2) * HALF + row * 2 + slot % 2


def whereabouts():
    domain, low = lax.axis_index("dom"), lax.axis_index("col")
    group, chain, core = domain // 4, (domain // 2) % 2, domain % 2
    odd = group % 2
    part = chain ^ low ^ odd
    base = (group * 4 + part * 2 + core) * ROWS
    return group, chain, core, low, odd, part, base


TO_RIGHT = ((5, 4, 3), (2, 1, 0))
TO_LEFT = ((0, 1, 2), (3, 4, 5))


def make_pack(own, pack):
    _, chain, core, low, odd, _, base = whereabouts()
    for right, (near, far) in ((True, TO_RIGHT), (False, TO_LEFT)):
        start = (core if right else 1 - core) * BOX
        for n in range(NEAR):
            pack[start + n] = own_flat(near[n // SLOTS], n % SLOTS)
        for depth, row in enumerate(far):
            count = jnp.int32(0)
            for n in range(3 - depth):
                pack[start + NEAR + FAR[depth] + n] = own_flat(row, 0)
            for slot in range(SLOTS):
                place = own[row, slot ^ (2 * low)] - base
                wanted = place >= 3 if right else place <= 2
                spot = start + NEAR + FAR[depth] + count
                pack[jnp.where(wanted, spot, 2 * BOX + 2)] = own_flat(row, slot)
                count = count + wanted.astype(jnp.int32)
    pack[2 * BOX] = chain
    pack[2 * BOX + 1] = (low == odd).astype(jnp.int32)


def make_table(inner, own, outer, table, place, spot):
    _, _, core, low, _, part, base = whereabouts()
    left_low = jnp.where((core == 0) & (part == 1), 1 - low, low)
    right_low = jnp.where((core == 1) & (part == 0), 1 - low, low)
    first = base - ROWS
    for row in range(ROWS):
        for slot in range(SLOTS):
            at = (ROWS + row) * SLOTS + slot
            place[at] = own[row, slot ^ (2 * low)] - first
            spot[at] = BOX + own_flat(row, slot)
    sides = (
        (core == 1, left_low, 0, (1 - core) * (BOX + OWN), TO_RIGHT),
        (core == 0, right_low, 2 * ROWS, core * (BOX + OWN), TO_LEFT),
    )
    for inside, swap, offset, start, (near, far) in sides:
        for depth, row in enumerate(near + far):
            count = jnp.int32(0)
            for slot in range(SLOTS):
                at = (offset + row) * SLOTS + slot
                column = slot ^ (2 * swap)
                value = jnp.where(inside, inner[row, column], outer[row, column]) - first
                place[at] = value
                if depth < 3:
                    spot[at] = start + depth * SLOTS + slot
                else:
                    wanted = value <= 14 if offset else value >= 3
                    found = start + NEAR + FAR[depth - 3] + count
                    spot[at] = jnp.where(wanted, found, ZERO)
                    count = count + wanted.astype(jnp.int32)

    def fill(row, carry):
        here = jnp.where(row < 6, row + 6, jnp.where(row < 9, row - 3, row + 3)) * SLOTS
        lists = [place[here + n] for n in range(SLOTS)]
        for t in range(SLOTS):
            inside = (lists[t] >= 0) & (lists[t] < 3 * ROWS)
            there = jnp.clip(lists[t], 0, 3 * ROWS - 1) * SLOTS
            found = [(place[there + u], spot[there + u]) for u in range(SLOTS)]
            for s in range(SLOTS):
                index = jnp.int32(ZERO)
                for column, block in found:
                    index = jnp.where(inside & (column == lists[s]), block, index)
                table[row * TAB + s * SLOTS + t] = index
            table[row * TAB + SLOTS * SLOTS + t] = spot[here + t]
        return carry

    lax.fori_loop(0, 2 * ROWS, fill, 0)


def bracket(table, row, operator, term, inverse):
    at = lambda n: table[row * TAB + n]
    mine = [at(SLOTS * SLOTS + t) for t in range(SLOTS)]
    pick = [[at(s * SLOTS + t) for s in range(SLOTS)] for t in range(SLOTS)]
    wide = lambda ref, places: jnp.concatenate([ref[n] for n in places], axis=1)
    left = jnp.concatenate([wide(operator, mine), -wide(term, mine)], axis=1)
    right = jnp.concatenate([wide(ref, p) for ref in (term, operator) for p in pick], axis=0)
    fresh = jnp.dot(left, right, preferred_element_type=jnp.float32)
    fresh = (fresh * inverse).astype(jnp.bfloat16)
    return mine, [fresh[:, s * BLOCK : (s + 1) * BLOCK] for s in range(SLOTS)]


def send_blocks(pack, source, to_inner, to_outer):
    for n in range(BOX):
        to_inner[n] = source[pack[n]]
        to_outer[n] = source[pack[BOX + n]]


def assemble(choose, pack, *refs):
    if choose:
        here, kept, turned_in, own, to_inner, to_outer = refs

        @pl.when(pack[2 * BOX + 1] == 1)
        def _():
            own[0:HALF] = here[...]

        @pl.when(pack[2 * BOX + 1] == 0)
        def _():
            own[0:HALF] = kept[...]

    else:
        kept, turned_in, own, to_inner, to_outer = refs
        own[0:HALF] = kept[...]
    own[HALF:OWN] = turned_in[...]
    send_blocks(pack, own, to_inner, to_outer)


def two_orders(order, last, table, pack, operator, own, inner, outer, *rest):
    if last:
        even_sum, odd_sum, kept, moved, term, first = rest
    else:
        first_out, second_out, to_inner, to_outer, term, first = rest
    zero = jnp.zeros((BLOCK, BLOCK), jnp.bfloat16)
    term[0:BOX] = inner[...]
    term[BOX : BOX + OWN] = own[...]
    term[BOX + OWN : ZERO] = outer[...]
    term[ZERO] = zero
    first[ZERO] = zero

    def first_row(row, carry):
        mine, blocks = bracket(table, row, operator, term, 1.0 / order)
        for n, block in zip(mine, blocks):
            first[n] = block
        return carry

    lax.fori_loop(0, 2 * ROWS, first_row, 0, unroll=UNROLL)

    if not last:
        first_out[...] = first[BOX : BOX + OWN]

    def second_row(row, carry):
        mine, blocks = bracket(table, row, operator, first, 1.0 / (order + 1))
        for n, block in zip(mine, blocks):
            if last:
                term[n] = block
            else:
                second_out[n - BOX] = block
        return carry

    lax.fori_loop(0, ROWS, second_row, 0, unroll=UNROLL)

    if not last:
        send_blocks(pack, second_out, to_inner, to_outer)
    else:
        chain = pack[2 * BOX]
        sign = jnp.where(chain == 0, -1.0, 1.0).astype(jnp.float32)

        def join(n, carry):
            for half, out in ((0, kept), (1, moved)):
                at = half * HALF + n
                even = even_sum[at] + WEIGHT[order + 1] * term[BOX + at].astype(jnp.float32)
                odd = odd_sum[at] + WEIGHT[order] * first[BOX + at].astype(jnp.float32)
                out[chain * HALF + n] = even.astype(jnp.bfloat16)
                out[(1 - chain) * HALF + n] = (sign * odd).astype(jnp.bfloat16)
            return carry

        lax.fori_loop(0, HALF, join, 0, unroll=4)


VMEM = pl.BlockSpec(memory_space=pltpu.VMEM)
SMEM = pl.BlockSpec(memory_space=pltpu.SMEM)


def blocks_of(count):
    return jax.ShapeDtypeStruct((count, BLOCK, BLOCK), jnp.bfloat16)


def run_pack(own):
    return pl.pallas_call(
        make_pack,
        out_shape=jax.ShapeDtypeStruct((2 * BOX + 3,), jnp.int32),
        in_specs=[SMEM],
        out_specs=SMEM,
        cost_estimate=pl.CostEstimate(flops=10**6, bytes_accessed=1024, transcendentals=0),
        name="make_pack",
    )(own)


def run_table(left, own, right):
    return pl.pallas_call(
        make_table,
        out_shape=jax.ShapeDtypeStruct((2 * ROWS * TAB,), jnp.int32),
        in_specs=[SMEM] * 3,
        out_specs=SMEM,
        scratch_shapes=[pltpu.SMEM((3 * ROWS * SLOTS,), jnp.int32)] * 2,
        cost_estimate=pl.CostEstimate(flops=10**6, bytes_accessed=1024, transcendentals=0),
        name="make_table",
    )(left, own, right)


def run_assemble(choose, pack, *pieces):
    return pl.pallas_call(
        functools.partial(assemble, choose),
        out_shape=(blocks_of(OWN), blocks_of(BOX), blocks_of(BOX)),
        in_specs=[SMEM] + [VMEM] * len(pieces),
        out_specs=(VMEM,) * 3,
        compiler_params=pltpu.CompilerParams(vmem_limit_bytes=16 * 1024 * 1024),
        cost_estimate=pl.CostEstimate(flops=0, bytes_accessed=3 * 2**20, transcendentals=0),
        name="assemble",
    )(pack, *pieces)


def run_orders(order, last, table, pack, operator, own, inner, outer, sums=()):
    sizes = (OWN, OWN) if last else (OWN, OWN, BOX, BOX)
    return pl.pallas_call(
        functools.partial(two_orders, order, last),
        out_shape=tuple(blocks_of(size) for size in sizes),
        in_specs=[SMEM] * 2 + [VMEM] * (4 + len(sums)),
        out_specs=(VMEM,) * len(sizes),
        scratch_shapes=[pltpu.VMEM((ZERO + 1, BLOCK, BLOCK), jnp.bfloat16)] * 2,
        compiler_params=pltpu.CompilerParams(vmem_limit_bytes=32 * 1024 * 1024),
        cost_estimate=pl.CostEstimate(
            flops=18 * 2 * 2 * 128 * 512 * 512, bytes_accessed=6 * 2**20, transcendentals=0
        ),
        name="two_orders",
    )(table, pack, operator, own, inner, outer, *sums)


def shards(groups, density, hamiltonian, neighbours):
    route = routes(groups)
    _, chain, _, low, odd, _, _ = whereabouts()
    move = functools.partial(lax.ppermute, axis_name=AXES)

    own_h = hamiltonian.reshape(HALF, BLOCK, BLOCK)
    own_lists = move(neighbours, perm=route["turn"])
    own_h, own_lists = lax.optimization_barrier((own_h, own_lists))
    first_side = move(own_lists, perm=route["inner"])
    second_side = move(own_lists, perm=route["outer"])
    turn_h = move(own_h, perm=route["turn"])
    keep_h = move(own_h, perm=route["keep"])
    turn_part = chain ^ low ^ 1 ^ odd
    turn_x = lax.dynamic_index_in_dim(density, turn_part, 0, False).reshape(HALF, BLOCK, BLOCK)
    here_x = lax.dynamic_index_in_dim(density, 1 - turn_part, 0, False).reshape(HALF, BLOCK, BLOCK)
    keep_x = move(here_x, perm=route["relay"])
    turn_x = move(turn_x, perm=route["turn"])
    keep_x = move(keep_x, perm=route["relay"])

    pack = run_pack(own_lists)
    operator, to_inner, to_outer = run_assemble(False, pack, keep_h, turn_h)
    table = run_table(first_side, own_lists, second_side)
    to_inner, to_outer, first_side, second_side = lax.optimization_barrier(
        (to_inner, to_outer, first_side, second_side)
    )
    outer = move(to_outer, perm=route["outer"])
    inner = move(to_inner, perm=route["inner"])
    zero = jnp.zeros((1, BLOCK, BLOCK), jnp.bfloat16)
    operator = jnp.concatenate([inner, operator, outer, zero], axis=0)

    term, to_inner, to_outer = run_assemble(True, pack, here_x, keep_x, turn_x)
    sums = [term.astype(jnp.float32) * WEIGHT[0], jnp.zeros((), jnp.float32)]
    count = STEPS * ORDERS
    for order in range(1, count, 2):
        outer = move(to_outer, perm=route["outer"])
        inner = move(to_inner, perm=route["inner"])
        if order + 1 == count:
            break
        first, term, to_inner, to_outer = run_orders(
            order, False, table, pack, operator, term, inner, outer
        )
        sums[1] = sums[1] + WEIGHT[order] * first.astype(jnp.float32)
        sums[0] = sums[0] + WEIGHT[order + 1] * term.astype(jnp.float32)
    kept, moved = run_orders(
        count - 1, True, table, pack, operator, term, inner, outer, tuple(sums)
    )
    kept = move(kept, perm=route["keep_back"])
    moved = move(moved, perm=route["turn_back"])
    total = kept.astype(jnp.float32) + moved.astype(jnp.float32)
    return total.reshape(density.shape)


def solution(mesh):
    placed = (P(None, "dom", "col", None, None), P("dom", "col", None, None), P("dom", None))
    return jax.shard_map(
        functools.partial(shards, mesh.shape["dom"] // 4),
        mesh=mesh,
        in_specs=placed,
        out_specs=P(None, "dom", "col", None, None),
        check_vma=False,
    )
```

time: 149 us -> 135 us (0.906)
  waiting for transfers between devices: 70.2 us -> 60.7 us
  local copies, waits for them, and re-layouts: 6.73 us -> 2.78 us
  starting transfers between devices: 39.6 us -> 42.4 us
  Pallas kernels: 26.8 us -> 24.7 us
    ppermute x16 -> x17, starting transfers between devices: 29 us -> 36.9 us  [the longest x5 29.6 us: shards(): outer = move(to_outer, perm=route['outer'])]
    ppermute x1, starting transfers between devices: 9.22 us -> 1.91 us  [shards(): keep_h = move(own_h, perm=route['keep'])]
    ppermute x16 -> x17, waiting for transfers between devices: 53.8 us -> 47.8 us  [the longest x5 25 us: shards(): outer = move(to_outer, perm=route['outer'])]
    ppermute x1, waiting for transfers between devices: 5.35 us -> 0.01 us  [shards(): turn_x = move(turn_x, perm=route['turn'])]
    ppermute x1, waiting for transfers between devices: 0.01 us -> 4.45 us  [shards(): turn_h = move(own_h, perm=route['turn'])]
    ppermute x1, starting transfers between devices: 0.08 us -> 3.46 us  [shards(): turn_x = move(turn_x, perm=route['turn'])]
    unnamed x9 -> x17, local copies, waits for them, and re-layouts: 3.37 us -> 0.73 us
    ppermute x1, waiting for transfers between devices: 11.1 us -> 8.47 us  [shards(): keep_h = move(own_h, perm=route['keep'])]
  transfers between devices with their start and end apart: 19 -> 20, of which waited for: 8 -> 9; matrix products, arithmetic and copies ran while one was open for 6% -> 2% of each run, Pallas kernels for 0% -> 5%
where the time goes in v2:
time: 135 us
  waiting for transfers between devices  60.7 us (45%)
  starting transfers between devices  42.4 us (31%)
  Pallas kernels  24.7 us (18%)
  other arithmetic  3.95 us (3%)
  local copies, waits for them, and re-layouts  2.78 us (2%)
    ppermute x5, starting transfers between devices, shards(): outer = move(to_outer, perm=route['outer'])  29.6 us
    ppermute x5, waiting for transfers between devices, shards(): outer = move(to_outer, perm=route['outer'])  25 us
    pallas_call x4, Pallas kernels, run_orders(): pl.pallas_call(functools.partial(two_orders, order, last), out_shape=tupl...  17.3 us
    ppermute x1, waiting for transfers between devices, shards(): moved = move(moved, perm=route['turn_back'])  12.5 us
    ppermute x1, waiting for transfers between devices, shards(): keep_h = move(own_h, perm=route['keep'])  8.47 us
    ppermute x1, waiting for transfers between devices, shards(): kept = move(kept, perm=route['keep_back'])  5.5 us
    ppermute x1, waiting for transfers between devices, shards(): own_lists = move(neighbours, perm=route['turn'])  4.75 us
    ppermute x1, waiting for transfers between devices, shards(): turn_h = move(own_h, perm=route['turn'])  4.45 us
  transfers between devices with their start and end apart: 20, of which 9 were waited for; matrix products, arithmetic and copies ran while one was open for 2% of the time, Pallas kernels for 5%

profile of v2, /device:TPU:24, one launch (start us, length us, event | category | flops | bytes accessed | tf_op | source)
XLA Modules:
  0.0 134.7 jit_solution(115687760061441238)
XLA Ops:
  0.0 2.0 %constant_dynamic-slice_fusion = (bf16[1,6,2,128,128]{4,3,2,1,0:T(8,128)(2,1)}, bf16[1,6,2,128,128]{4,3,2,1,0:T(8,128)(2,1)S(1)}) fusion(bf16[2,6,2,128,128]{4,3,2,1,0:T(8,128)(2,1)} %param.3, s32[]{:T(128)S(6)} %select_n.30, s32[]{:T(128)S(6)} %select_n.29), kind=kLoop, calls=%fused_computation.4 | loop fusion | bytes 1572872 | tf_op jit(solution)/shard_map/jit(dynamic_index_in_dim)/dynamic_slice | solution.py:329
  2.0 2.0 %collective-permute-start.7 = (bf16[12,128,128]{2,1,0:T(8,128)(2,1)S(1)}, bf16[12,128,128]{2,1,0:T(8,128)(2,1)}, u32[]{:S(2)}, u32[]{:S(2)}) collective-permute-start(bf16[12,128,128]{2,1,0:T(8,128)(2,1)S(1)} %bitcast.5), channel_id=1, source_target_pairs={{0,1},{1,4},{2,3},{3,6},{4,5},{5,0},{6,7},{7,2},{8,13},{9,8},{10,1... | collective-permute-start | bytes 1179656 | tf_op jit(solution)/shard_map/ppermute | solution.py:331
  4.1 4.7 %collective-permute-done.own = s32[6,4]{1,0:T(8,128)S(1)} collective-permute-done((s32[6,4]{1,0:T(8,128)S(1)}, s32[6,4]{1,0:T(8,128)S(1)}, u32[]{:S(2)}, u32[]{:S(2)}) %collective-permute-start) | collective-permute-done | bytes 128 | tf_op jit(solution)/shard_map/ppermute | solution.py:322
  8.9 1.9 %collective-permute-start.3 = (bf16[12,128,128]{2,1,0:T(8,128)(2,1)S(1)}, bf16[12,128,128]{2,1,0:T(8,128)(2,1)S(1)}, u32[]{:S(2)}, u32[]{:S(2)}) collective-permute-start(bf16[12,128,128]{2,1,0:T(8,128)(2,1)S(1)} %bitcast.7), channel_id=1, source_target_pairs={{0,0},{1,5},{2,2},{3,7},{4,4},{5,1},{6,6},{7,3},{8,12},{9,9},{10,1... | collective-permute-start | bytes 1179656 | tf_op jit(solution)/shard_map/ppermute | solution.py:327
  10.9 3.5 %collective-permute-start.9 = (bf16[12,128,128]{2,1,0:T(8,128)(2,1)}, bf16[12,128,128]{2,1,0:T(8,128)(2,1)S(1)}, u32[]{:S(2)}, u32[]{:S(2)}) collective-permute-start(bf16[12,128,128]{2,1,0:T(8,128)(2,1)} %bitcast.2), channel_id=1, source_target_pairs={{0,5},{1,0},{2,7},{3,2},{4,1},{5,4},{6,3},{7,6},{8,9},{9,12},{10,1... | collective-permute-start | bytes 1179656 | tf_op jit(solution)/shard_map/ppermute | solution.py:332
  14.4 1.4 %make_pack.1.pack = s32[39]{0:T(128)} custom-call(s32[6,4]{1,0:T(8,128)} %copy-done.3), custom_call_target="tpu_custom_call" | custom-call | flops 1000000 | bytes 1024 | tf_op jit(solution)/shard_map/make_pack/pallas_call | solution.py:266
  15.8 8.5 %collective-permute-done.3.refs_0_ = bf16[12,128,128]{2,1,0:T(8,128)(2,1)S(1)} collective-permute-done((bf16[12,128,128]{2,1,0:T(8,128)(2,1)S(1)}, bf16[12,128,128]{2,1,0:T(8,128)(2,1)S(1)}, u32[]{:S(2)}, u32[]{:S(2)}) %collective-permute-start.3) | collective-permute-done | bytes 393248 | tf_op jit(solution)/shard_map/ppermute | solution.py:327
  24.3 4.5 %collective-permute-done.4.refs_1_ = bf16[12,128,128]{2,1,0:T(8,128)(2,1)S(1)} collective-permute-done((bf16[12,128,128]{2,1,0:T(8,128)(2,1)S(1)}, bf16[12,128,128]{2,1,0:T(8,128)(2,1)S(1)}, u32[]{:S(2)}, u32[]{:S(2)}) %collective-permute-start.4) | collective-permute-done | bytes 393248 | tf_op jit(solution)/shard_map/ppermute | solution.py:326
  28.8 0.6 copy-done
  29.4 1.5 %assemble.2 = (bf16[24,128,128]{2,1,0:T(8,128)(2,1)S(1)}, bf16[18,128,128]{2,1,0:T(8,128)(2,1)S(1)}, bf16[18,128,128]{2,1,0:T(8,128)(2,1)}) custom-call(s32[39]{0:T(128)S(1)} %copy-done, bf16[12,128,128]{2,1,0:T(8,128)(2,1)S(1)} %collective-permute-done.3.refs_0_, bf16[12,128,128]{2,1,0:T(8,128)(2,1)S(1)} %collective-permute-done.4.refs_1_), custom_call_target="tpu_custom_call" | custom-call | bytes 3145728 | tf_op jit(solution)/shard_map/assemble/pallas_call | solution.py:289
  30.9 6.3 %collective-permute-start.6 = (bf16[18,128,128]{2,1,0:T(8,128)(2,1)}, bf16[18,128,128]{2,1,0:T(8,128)(2,1)}, u32[]{:S(2)}, u32[]{:S(2)}) collective-permute-start(bf16[18,128,128]{2,1,0:T(8,128)(2,1)} %get-tuple-element.35), channel_id=1, source_target_pairs={{0,250},{1,2},{2,1},{3,9},{4,7},{5,255},{6,12},{7,4},{8,11},{9,3},... | collective-permute-start | bytes 1769480 | tf_op jit(solution)/shard_map/ppermute | solution.py:341
  37.2 1.7 %assemble.3 = (bf16[24,128,128]{2,1,0:T(8,128)(2,1)S(1)}, bf16[18,128,128]{2,1,0:T(8,128)(2,1)}, bf16[18,128,128]{2,1,0:T(8,128)(2,1)}) custom-call(s32[39]{0:T(128)S(1)} %copy-done, bf16[12,128,128]{2,1,0:T(8,128)(2,1)S(1)} %bitcast.6, bf16[12,128,128]{2,1,0:T(8,128)(2,1)S(1)} %collective-permute-done.8.refs_1_, ...), custom_call_target="tpu_custom_call" | custom-call | bytes 3145728 | tf_op jit(solution)/shard_map/assemble/pallas_call | solution.py:289
  39.4 7.7 %collective-permute-start.11 = (bf16[18,128,128]{2,1,0:T(8,128)(2,1)}, bf16[18,128,128]{2,1,0:T(8,128)(2,1)}, u32[]{:S(2)}, u32[]{:S(2)}) collective-permute-start(bf16[18,128,128]{2,1,0:T(8,128)(2,1)} %get-tuple-element.38), channel_id=1, source_target_pairs={{0,250},{1,2},{2,1},{3,9},{4,7},{5,255},{6,12},{7,4},{8,11},{9,3},... | collective-permute-start | bytes 1769480 | tf_op jit(solution)/shard_map/ppermute | solution.py:350
  47.2 2.8 %make_table.1.table = s32[240]{0:T(256)} custom-call(s32[6,4]{1,0:T(8,128)} %copy-done.4, s32[6,4]{1,0:T(8,128)} %copy-done.3, s32[6,4]{1,0:T(8,128)} %copy-done.5), custom_call_target="tpu_custom_call" | custom-call | flops 1000000 | bytes 1024 | tf_op jit(solution)/shard_map/make_table/pallas_call | solution.py:277
  50.1 1.5 %maximum_maximum_fusion.operator = bf16[61,128,128]{2,1,0:T(8,128)(2,1)S(1)} fusion(bf16[18,128,128]{2,1,0:T(8,128)(2,1)} %collective-permute-done.6, bf16[24,128,128]{2,1,0:T(8,128)(2,1)S(1)} %get-tuple-element.34, bf16[18,128,128]{2,1,0:T(8,128)(2,1)} %collective-permute-done.5, bf16[61]{0:T(256)(128)(2,1)S(1)} %pad.3.clone), kind=kLoop, calls=%fused_computation | loop fusion | flops 2998272 | bytes 3965050 | tf_op jit(solution)/shard_map/concatenate | solution.py:344
  51.6 3.4 %collective-permute-done.11.outer = bf16[18,128,128]{2,1,0:T(8,128)(2,1)} collective-permute-done((bf16[18,128,128]{2,1,0:T(8,128)(2,1)}, bf16[18,128,128]{2,1,0:T(8,128)(2,1)}, u32[]{:S(2)}, u32[]{:S(2)}) %collective-permute-start.11) | collective-permute-done | bytes 589856 | tf_op jit(solution)/shard_map/ppermute | solution.py:350
  55.0 4.9 %two_orders.4 = (bf16[24,128,128]{2,1,0:T(8,128)(2,1)S(1)}, bf16[24,128,128]{2,1,0:T(8,128)(2,1)S(1)}, bf16[18,128,128]{2,1,0:T(8,128)(2,1)S(1)}, bf16[18,128,128]{2,1,0:T(8,128)(2,1)S(1)}) custom-call(s32[240]{0:T(256)S(1)} %copy-done.2, s32[39]{0:T(128)S(1)} %copy-done.1, bf16[61,128,128]{2,1,0:T(8,128)(2,1)S(1)} %maximum_maximum_fusion.operator, ...), custom_call_target="tpu_custom_call" | custom-call | flops 2415919104 | bytes 6291456 | tf_op jit(solution)/shard_map/two_orders/pallas_call | solution.py:302
  60.0 5.3 %collective-permute-start.13 = (bf16[18,128,128]{2,1,0:T(8,128)(2,1)S(1)}, bf16[18,128,128]{2,1,0:T(8,128)(2,1)S(1)}, u32[]{:S(2)}, u32[]{:S(2)}) collective-permute-start(bf16[18,128,128]{2,1,0:T(8,128)(2,1)S(1)} %get-tuple-element.41), channel_id=1, source_target_pairs={{0,250},{1,2},{2,1},{3,9},{4,7},{5,255},{6,12},{7,4},{8,11},{9,3},... | collective-permute-start | bytes 1769480 | tf_op jit(solution)/shard_map/ppermute | solution.py:350
  65.3 7.6 %collective-permute-done.13.outer = bf16[18,128,128]{2,1,0:T(8,128)(2,1)S(1)} collective-permute-done((bf16[18,128,128]{2,1,0:T(8,128)(2,1)S(1)}, bf16[18,128,128]{2,1,0:T(8,128)(2,1)S(1)}, u32[]{:S(2)}, u32[]{:S(2)}) %collective-permute-start.13) | collective-permute-done | bytes 589856 | tf_op jit(solution)/shard_map/ppermute | solution.py:350
  72.9 4.1 %two_orders.5 = (bf16[24,128,128]{2,1,0:T(8,128)(2,1)S(1)}, bf16[24,128,128]{2,1,0:T(8,128)(2,1)S(1)}, bf16[18,128,128]{2,1,0:T(8,128)(2,1)S(1)}, bf16[18,128,128]{2,1,0:T(8,128)(2,1)S(1)}) custom-call(s32[240]{0:T(256)S(1)} %copy-done.2, s32[39]{0:T(128)S(1)} %copy-done.1, bf16[61,128,128]{2,1,0:T(8,128)(2,1)S(1)} %maximum_maximum_fusion.operator, ...), custom_call_target="tpu_custom_call" | custom-call | flops 2415919104 | bytes 6291456 | tf_op jit(solution)/shard_map/two_orders/pallas_call | solution.py:302
  77.1 5.1 %collective-permute-start.15 = (bf16[18,128,128]{2,1,0:T(8,128)(2,1)S(1)}, bf16[18,128,128]{2,1,0:T(8,128)(2,1)S(1)}, u32[]{:S(2)}, u32[]{:S(2)}) collective-permute-start(bf16[18,128,128]{2,1,0:T(8,128)(2,1)S(1)} %get-tuple-element.44), channel_id=1, source_target_pairs={{0,250},{1,2},{2,1},{3,9},{4,7},{5,255},{6,12},{7,4},{8,11},{9,3},... | collective-permute-start | bytes 1769480 | tf_op jit(solution)/shard_map/ppermute | solution.py:350
  82.2 7.6 %collective-permute-done.15.outer = bf16[18,128,128]{2,1,0:T(8,128)(2,1)S(1)} collective-permute-done((bf16[18,128,128]{2,1,0:T(8,128)(2,1)S(1)}, bf16[18,128,128]{2,1,0:T(8,128)(2,1)S(1)}, u32[]{:S(2)}, u32[]{:S(2)}) %collective-permute-start.15) | collective-permute-done | bytes 589856 | tf_op jit(solution)/shard_map/ppermute | solution.py:350
  89.8 4.0 %two_orders.6 = (bf16[24,128,128]{2,1,0:T(8,128)(2,1)S(1)}, bf16[24,128,128]{2,1,0:T(8,128)(2,1)S(1)}, bf16[18,128,128]{2,1,0:T(8,128)(2,1)S(1)}, bf16[18,128,128]{2,1,0:T(8,128)(2,1)S(1)}) custom-call(s32[240]{0:T(256)S(1)} %copy-done.2, s32[39]{0:T(128)S(1)} %copy-done.1, bf16[61,128,128]{2,1,0:T(8,128)(2,1)S(1)} %maximum_maximum_fusion.operator, ...), custom_call_target="tpu_custom_call" | custom-call | flops 2415919104 | bytes 6291456 | tf_op jit(solution)/shard_map/two_orders/pallas_call | solution.py:302
  93.8 5.1 %collective-permute-start.17 = (bf16[18,128,128]{2,1,0:T(8,128)(2,1)S(1)}, bf16[18,128,128]{2,1,0:T(8,128)(2,1)S(1)}, u32[]{:S(2)}, u32[]{:S(2)}) collective-permute-start(bf16[18,128,128]{2,1,0:T(8,128)(2,1)S(1)} %get-tuple-element.47), channel_id=1, source_target_pairs={{0,250},{1,2},{2,1},{3,9},{4,7},{5,255},{6,12},{7,4},{8,11},{9,3},... | collective-permute-start | bytes 1769480 | tf_op jit(solution)/shard_map/ppermute | solution.py:350
  99.0 1.1 multiply_add_fusion
  100.1 6.5 %collective-permute-done.17.outer = bf16[18,128,128]{2,1,0:T(8,128)(2,1)S(1)} collective-permute-done((bf16[18,128,128]{2,1,0:T(8,128)(2,1)S(1)}, bf16[18,128,128]{2,1,0:T(8,128)(2,1)S(1)}, u32[]{:S(2)}, u32[]{:S(2)}) %collective-permute-start.17) | collective-permute-done | bytes 589856 | tf_op jit(solution)/shard_map/ppermute | solution.py:350
  106.6 4.4 %two_orders.7 = (bf16[24,128,128]{2,1,0:T(8,128)(2,1)S(1)}, bf16[24,128,128]{2,1,0:T(8,128)(2,1)S(1)}) custom-call(s32[240]{0:T(256)S(1)} %copy-done.2, s32[39]{0:T(128)S(1)} %copy-done.1, bf16[61,128,128]{2,1,0:T(8,128)(2,1)S(1)} %maximum_maximum_fusion.operator, bf16[24,128,128]{2,1,0:T(8,128)(2,1)S(1)} %get-tuple-element.45.own, ...), custom_call_target="tpu_custom_call" | custom-call | flops 2415919104 | bytes 6291456 | tf_op jit(solution)/shard_map/two_orders/pallas_call | solution.py:302
  111.0 2.5 %collective-permute-start.19 = (bf16[24,128,128]{2,1,0:T(8,128)(2,1)S(1)}, bf16[24,128,128]{2,1,0:T(8,128)(2,1)S(1)}, u32[]{:S(2)}, u32[]{:S(2)}) collective-permute-start(bf16[24,128,128]{2,1,0:T(8,128)(2,1)S(1)} %get-tuple-element.52), channel_id=1, source_target_pairs={{0,1},{1,4},{2,3},{3,6},{4,5},{5,0},{6,7},{7,2},{8,13},{9,8},{10,1... | collective-permute-start | bytes 2359304 | tf_op jit(solution)/shard_map/ppermute | solution.py:363
  113.4 1.9 %collective-permute-start.18 = (bf16[24,128,128]{2,1,0:T(8,128)(2,1)S(1)}, bf16[24,128,128]{2,1,0:T(8,128)(2,1)S(1)}, u32[]{:S(2)}, u32[]{:S(2)}) collective-permute-start(bf16[24,128,128]{2,1,0:T(8,128)(2,1)S(1)} %get-tuple-element.51), channel_id=1, source_target_pairs={{0,0},{1,5},{2,2},{3,7},{4,4},{5,1},{6,6},{7,3},{8,12},{9,9},{10,1... | collective-permute-start | bytes 2359304 | tf_op jit(solution)/shard_map/ppermute | solution.py:362
  115.4 12.5 %collective-permute-done.19 = bf16[24,128,128]{2,1,0:T(8,128)(2,1)S(1)} collective-permute-done((bf16[24,128,128]{2,1,0:T(8,128)(2,1)S(1)}, bf16[24,128,128]{2,1,0:T(8,128)(2,1)S(1)}, u32[]{:S(2)}, u32[]{:S(2)}) %collective-permute-start.19) | collective-permute-done | bytes 786464 | tf_op jit(solution)/shard_map/ppermute | solution.py:363
  127.9 5.5 %collective-permute-done.18 = bf16[24,128,128]{2,1,0:T(8,128)(2,1)S(1)} collective-permute-done((bf16[24,128,128]{2,1,0:T(8,128)(2,1)S(1)}, bf16[24,128,128]{2,1,0:T(8,128)(2,1)S(1)}, u32[]{:S(2)}, u32[]{:S(2)}) %collective-permute-start.18) | collective-permute-done | bytes 786464 | tf_op jit(solution)/shard_map/ppermute | solution.py:362
  133.4 1.4 %convert_add_fusion = f32[24,128,128]{2,1,0:T(8,128)} fusion(bf16[24,128,128]{2,1,0:T(8,128)(2,1)S(1)} %collective-permute-done.19, bf16[24,128,128]{2,1,0:T(8,128)(2,1)S(1)} %collective-permute-done.18), kind=kLoop, calls=%fused_computation.1 | loop fusion | flops 1179648 | bytes 3145728 | tf_op jit(solution)/shard_map/add | solution.py:364
  (38 shorter events, 1.3 us)
Async XLA Ops:
  0.0 3.9 %copy-start.6 = (s32[6,4]{0,1:T(4,128)S(1)}, s32[6,4]{0,1:T(4,128)}, u32[]{:S(2)}) copy-start(s32[6,4]{0,1:T(4,128)} %param.5) | copy-start | bytes 292
  0.0 8.9 %copy-start.7 = (bf16[6,2,128,128]{3,2,1,0:T(8,128)(2,1)S(1)}, bf16[6,2,128,128]{3,2,1,0:T(8,128)(2,1)}, u32[]{:S(2)}) copy-start(bf16[6,2,128,128]{3,2,1,0:T(8,128)(2,1)} %param.4) | copy-start | bytes 1179652
  2.0 12.4 %collective-permute-start.7 = (bf16[12,128,128]{2,1,0:T(8,128)(2,1)S(1)}, bf16[12,128,128]{2,1,0:T(8,128)(2,1)}, u32[]{:S(2)}, u32[]{:S(2)}) collective-permute-start(bf16[12,128,128]{2,1,0:T(8,128)(2,1)S(1)} %bitcast.5), channel_id=1, source_target_pairs={{0,1},{1,4},{2,3},{3,6},{4,5},{5,0},{6,7},{7,2},{8,13},{9,8},{10,1... | collective-permute-start | bytes 1179656 | tf_op jit(solution)/shard_map/ppermute | solution.py:331
  4.0 4.8 %collective-permute-start = (s32[6,4]{1,0:T(8,128)S(1)}, s32[6,4]{1,0:T(8,128)S(1)}, u32[]{:S(2)}, u32[]{:S(2)}) collective-permute-start(s32[6,4]{1,0:T(8,128)S(1)} %copy.4), channel_id=1, source_target_pairs={{0,5},{1,0},{2,7},{3,2},{4,1},{5,4},{6,3},{7,6},{8,9},{9,12},{10,1... | collective-permute-start | bytes 296 | tf_op jit(solution)/shard_map/ppermute | solution.py:322
  8.9 5.6 %copy-start.3 = (s32[6,4]{1,0:T(8,128)}, s32[6,4]{1,0:T(8,128)S(1)}, u32[]{:S(2)}) copy-start(s32[6,4]{1,0:T(8,128)S(1)} %collective-permute-done.own) | copy-start | bytes 292
  8.9 15.4 %collective-permute-start.3 = (bf16[12,128,128]{2,1,0:T(8,128)(2,1)S(1)}, bf16[12,128,128]{2,1,0:T(8,128)(2,1)S(1)}, u32[]{:S(2)}, u32[]{:S(2)}) collective-permute-start(bf16[12,128,128]{2,1,0:T(8,128)(2,1)S(1)} %bitcast.7), channel_id=1, source_target_pairs={{0,0},{1,5},{2,2},{3,7},{4,4},{5,1},{6,6},{7,3},{8,12},{9,9},{10,1... | collective-permute-start | bytes 1179656 | tf_op jit(solution)/shard_map/ppermute | solution.py:327
  10.8 18.0 %collective-permute-start.4 = (bf16[12,128,128]{2,1,0:T(8,128)(2,1)S(1)}, bf16[12,128,128]{2,1,0:T(8,128)(2,1)S(1)}, u32[]{:S(2)}, u32[]{:S(2)}) collective-permute-start(bf16[12,128,128]{2,1,0:T(8,128)(2,1)S(1)} %bitcast.8), channel_id=1, source_target_pairs={{0,5},{1,0},{2,7},{3,2},{4,1},{5,4},{6,3},{7,6},{8,9},{9,12},{10,1... | collective-permute-start | bytes 1179656 | tf_op jit(solution)/shard_map/ppermute | solution.py:326
  10.9 26.3 %collective-permute-start.9 = (bf16[12,128,128]{2,1,0:T(8,128)(2,1)}, bf16[12,128,128]{2,1,0:T(8,128)(2,1)S(1)}, u32[]{:S(2)}, u32[]{:S(2)}) collective-permute-start(bf16[12,128,128]{2,1,0:T(8,128)(2,1)} %bitcast.2), channel_id=1, source_target_pairs={{0,5},{1,0},{2,7},{3,2},{4,1},{5,4},{6,3},{7,6},{8,9},{9,12},{10,1... | collective-permute-start | bytes 1179656 | tf_op jit(solution)/shard_map/ppermute | solution.py:332
  14.3 22.9 %collective-permute-start.8 = (bf16[12,128,128]{2,1,0:T(8,128)(2,1)}, bf16[12,128,128]{2,1,0:T(8,128)(2,1)S(1)}, u32[]{:S(2)}, u32[]{:S(2)}) collective-permute-start(bf16[12,128,128]{2,1,0:T(8,128)(2,1)} %collective-permute-done.7), channel_id=1, source_target_pairs={{0,1},{1,4},{2,3},{3,6},{4,5},{5,0},{6,7},{7,2},{8,13},{9,8},{10,1... | collective-permute-start | bytes 1179656 | tf_op jit(solution)/shard_map/ppermute | solution.py:333
  14.4 16.4 %collective-permute-start.1 = (s32[6,4]{1,0:T(8,128)S(1)}, s32[6,4]{1,0:T(8,128)S(1)}, u32[]{:S(2)}, u32[]{:S(2)}) collective-permute-start(s32[6,4]{1,0:T(8,128)S(1)} %collective-permute-done.own), channel_id=1, source_target_pairs={{0,2},{1,3},{2,0},{3,1},{4,6},{5,7},{6,4},{7,5},{8,10},{9,11},{10,... | collective-permute-start | bytes 296 | tf_op jit(solution)/shard_map/ppermute | solution.py:324
  24.3 6.6 %collective-permute-start.2 = (s32[6,4]{1,0:T(8,128)}, s32[6,4]{1,0:T(8,128)S(1)}, u32[]{:S(2)}, u32[]{:S(2)}) collective-permute-start(s32[6,4]{1,0:T(8,128)} %copy-done.3), channel_id=1, source_target_pairs={{0,250},{1,2},{2,1},{3,9},{4,7},{5,255},{6,12},{7,4},{8,11},{9,3},... | collective-permute-start | bytes 296 | tf_op jit(solution)/shard_map/ppermute | solution.py:325
  28.8 0.6 copy-start
  30.9 16.3 %copy-start.4 = (s32[6,4]{1,0:T(8,128)}, s32[6,4]{1,0:T(8,128)S(1)}, u32[]{:S(2)}) copy-start(s32[6,4]{1,0:T(8,128)S(1)} %collective-permute-done.1.inner) | copy-start | bytes 292
  30.9 16.3 %copy-start.5 = (s32[6,4]{1,0:T(8,128)}, s32[6,4]{1,0:T(8,128)S(1)}, u32[]{:S(2)}) copy-start(s32[6,4]{1,0:T(8,128)S(1)} %collective-permute-done.2.outer) | copy-start | bytes 292
  30.9 19.2 %collective-permute-start.6 = (bf16[18,128,128]{2,1,0:T(8,128)(2,1)}, bf16[18,128,128]{2,1,0:T(8,128)(2,1)}, u32[]{:S(2)}, u32[]{:S(2)}) collective-permute-start(bf16[18,128,128]{2,1,0:T(8,128)(2,1)} %get-tuple-element.35), channel_id=1, source_target_pairs={{0,250},{1,2},{2,1},{3,9},{4,7},{5,255},{6,12},{7,4},{8,11},{9,3},... | collective-permute-start | bytes 1769480 | tf_op jit(solution)/shard_map/ppermute | solution.py:341
  37.2 12.8 %collective-permute-start.5 = (bf16[18,128,128]{2,1,0:T(8,128)(2,1)S(1)}, bf16[18,128,128]{2,1,0:T(8,128)(2,1)}, u32[]{:S(2)}, u32[]{:S(2)}) collective-permute-start(bf16[18,128,128]{2,1,0:T(8,128)(2,1)S(1)} %get-tuple-element.33), channel_id=1, source_target_pairs={{0,2},{1,3},{2,0},{3,1},{4,6},{5,7},{6,4},{7,5},{8,10},{9,11},{10,... | collective-permute-start | bytes 1769480 | tf_op jit(solution)/shard_map/ppermute | solution.py:342
  38.9 12.7 %collective-permute-start.10 = (bf16[18,128,128]{2,1,0:T(8,128)(2,1)}, bf16[18,128,128]{2,1,0:T(8,128)(2,1)S(1)}, u32[]{:S(2)}, u32[]{:S(2)}) collective-permute-start(bf16[18,128,128]{2,1,0:T(8,128)(2,1)} %get-tuple-element.37), channel_id=1, source_target_pairs={{0,2},{1,3},{2,0},{3,1},{4,6},{5,7},{6,4},{7,5},{8,10},{9,11},{10,... | collective-permute-start | bytes 1769480 | tf_op jit(solution)/shard_map/ppermute | solution.py:351
  39.4 15.6 %collective-permute-start.11 = (bf16[18,128,128]{2,1,0:T(8,128)(2,1)}, bf16[18,128,128]{2,1,0:T(8,128)(2,1)}, u32[]{:S(2)}, u32[]{:S(2)}) collective-permute-start(bf16[18,128,128]{2,1,0:T(8,128)(2,1)} %get-tuple-element.38), channel_id=1, source_target_pairs={{0,250},{1,2},{2,1},{3,9},{4,7},{5,255},{6,12},{7,4},{8,11},{9,3},... | collective-permute-start | bytes 1769480 | tf_op jit(solution)/shard_map/ppermute | solution.py:350
  50.0 4.9 %copy-start.1 = (s32[39]{0:T(128)S(1)}, s32[39]{0:T(128)}, u32[]{:S(2)}) copy-start(s32[39]{0:T(128)} %make_pack.1.pack) | copy-start | bytes 472
  50.0 4.9 %copy-start.2 = (s32[240]{0:T(256)S(1)}, s32[240]{0:T(256)}, u32[]{:S(2)}) copy-start(s32[240]{0:T(256)} %make_table.1.table) | copy-start | bytes 2884
  59.9 5.4 %collective-permute-start.12 = (bf16[18,128,128]{2,1,0:T(8,128)(2,1)S(1)}, bf16[18,128,128]{2,1,0:T(8,128)(2,1)S(1)}, u32[]{:S(2)}, u32[]{:S(2)}) collective-permute-start(bf16[18,128,128]{2,1,0:T(8,128)(2,1)S(1)} %get-tuple-element.40), channel_id=1, source_target_pairs={{0,2},{1,3},{2,0},{3,1},{4,6},{5,7},{6,4},{7,5},{8,10},{9,11},{10,... | collective-permute-start | bytes 1769480 | tf_op jit(solution)/shard_map/ppermute | solution.py:351
  60.0 12.9 %collective-permute-start.13 = (bf16[18,128,128]{2,1,0:T(8,128)(2,1)S(1)}, bf16[18,128,128]{2,1,0:T(8,128)(2,1)S(1)}, u32[]{:S(2)}, u32[]{:S(2)}) collective-permute-start(bf16[18,128,128]{2,1,0:T(8,128)(2,1)S(1)} %get-tuple-element.41), channel_id=1, source_target_pairs={{0,250},{1,2},{2,1},{3,9},{4,7},{5,255},{6,12},{7,4},{8,11},{9,3},... | collective-permute-start | bytes 1769480 | tf_op jit(solution)/shard_map/ppermute | solution.py:350
  77.0 5.2 %collective-permute-start.14 = (bf16[18,128,128]{2,1,0:T(8,128)(2,1)S(1)}, bf16[18,128,128]{2,1,0:T(8,128)(2,1)S(1)}, u32[]{:S(2)}, u32[]{:S(2)}) collective-permute-start(bf16[18,128,128]{2,1,0:T(8,128)(2,1)S(1)} %get-tuple-element.43), channel_id=1, source_target_pairs={{0,2},{1,3},{2,0},{3,1},{4,6},{5,7},{6,4},{7,5},{8,10},{9,11},{10,... | collective-permute-start | bytes 1769480 | tf_op jit(solution)/shard_map/ppermute | solution.py:351
  77.1 12.7 %collective-permute-start.15 = (bf16[18,128,128]{2,1,0:T(8,128)(2,1)S(1)}, bf16[18,128,128]{2,1,0:T(8,128)(2,1)S(1)}, u32[]{:S(2)}, u32[]{:S(2)}) collective-permute-start(bf16[18,128,128]{2,1,0:T(8,128)(2,1)S(1)} %get-tuple-element.44), channel_id=1, source_target_pairs={{0,250},{1,2},{2,1},{3,9},{4,7},{5,255},{6,12},{7,4},{8,11},{9,3},... | collective-permute-start | bytes 1769480 | tf_op jit(solution)/shard_map/ppermute | solution.py:350
  93.7 6.3 %collective-permute-start.16 = (bf16[18,128,128]{2,1,0:T(8,128)(2,1)S(1)}, bf16[18,128,128]{2,1,0:T(8,128)(2,1)S(1)}, u32[]{:S(2)}, u32[]{:S(2)}) collective-permute-start(bf16[18,128,128]{2,1,0:T(8,128)(2,1)S(1)} %get-tuple-element.46), channel_id=1, source_target_pairs={{0,2},{1,3},{2,0},{3,1},{4,6},{5,7},{6,4},{7,5},{8,10},{9,11},{10,... | collective-permute-start | bytes 1769480 | tf_op jit(solution)/shard_map/ppermute | solution.py:351
  93.8 12.7 %collective-permute-start.17 = (bf16[18,128,128]{2,1,0:T(8,128)(2,1)S(1)}, bf16[18,128,128]{2,1,0:T(8,128)(2,1)S(1)}, u32[]{:S(2)}, u32[]{:S(2)}) collective-permute-start(bf16[18,128,128]{2,1,0:T(8,128)(2,1)S(1)} %get-tuple-element.47), channel_id=1, source_target_pairs={{0,250},{1,2},{2,1},{3,9},{4,7},{5,255},{6,12},{7,4},{8,11},{9,3},... | collective-permute-start | bytes 1769480 | tf_op jit(solution)/shard_map/ppermute | solution.py:350
  111.0 16.9 %collective-permute-start.19 = (bf16[24,128,128]{2,1,0:T(8,128)(2,1)S(1)}, bf16[24,128,128]{2,1,0:T(8,128)(2,1)S(1)}, u32[]{:S(2)}, u32[]{:S(2)}) collective-permute-start(bf16[24,128,128]{2,1,0:T(8,128)(2,1)S(1)} %get-tuple-element.52), channel_id=1, source_target_pairs={{0,1},{1,4},{2,3},{3,6},{4,5},{5,0},{6,7},{7,2},{8,13},{9,8},{10,1... | collective-permute-start | bytes 2359304 | tf_op jit(solution)/shard_map/ppermute | solution.py:363
  113.4 19.9 %collective-permute-start.18 = (bf16[24,128,128]{2,1,0:T(8,128)(2,1)S(1)}, bf16[24,128,128]{2,1,0:T(8,128)(2,1)S(1)}, u32[]{:S(2)}, u32[]{:S(2)}) collective-permute-start(bf16[24,128,128]{2,1,0:T(8,128)(2,1)S(1)} %get-tuple-element.51), channel_id=1, source_target_pairs={{0,0},{1,5},{2,2},{3,7},{4,4},{5,1},{6,6},{7,3},{8,12},{9,9},{10,1... | collective-permute-start | bytes 2359304 | tf_op jit(solution)/shard_map/ppermute | solution.py:362

commit v3 on v2

--- a/solution.py
+++ b/solution.py
@@ -35,7 +35,7 @@
 BOX = NEAR + 6
 ZERO = 2 * BOX + OWN
 TAB = 20
-UNROLL = 6
+UNROLL = 12
 
 
 def flat_of(group, y, core):
@@ -234,7 +234,7 @@
                 second_out[n - BOX] = block
         return carry
 
-    lax.fori_loop(0, ROWS, second_row, 0, unroll=UNROLL)
+    lax.fori_loop(0, ROWS, second_row, 0, unroll=ROWS)
 
     if not last:
         send_blocks(pack, second_out, to_inner, to_outer)
@@ -320,12 +320,12 @@
 
     own_h = hamiltonian.reshape(HALF, BLOCK, BLOCK)
     own_lists = move(neighbours, perm=route["turn"])
-    own_h, own_lists = lax.optimization_barrier((own_h, own_lists))
+    turn_part = chain ^ low ^ 1 ^ odd
+    own_h, own_lists, turn_part = lax.optimization_barrier((own_h, own_lists, turn_part))
     first_side = move(own_lists, perm=route["inner"])
     second_side = move(own_lists, perm=route["outer"])
     turn_h = move(own_h, perm=route["turn"])
     keep_h = move(own_h, perm=route["keep"])
-    turn_part = chain ^ low ^ 1 ^ odd
     turn_x = lax.dynamic_index_in_dim(density, turn_part, 0, False).reshape(HALF, BLOCK, BLOCK)
     here_x = lax.dynamic_index_in_dim(density, 1 - turn_part, 0, False).reshape(HALF, BLOCK, BLOCK)
     keep_x = move(here_x, perm=route["relay"])

time: 135 us -> 134 us (level)
  waiting for transfers between devices: 60.7 us -> 56.6 us
  starting transfers between devices: 42.4 us -> 45.4 us
    ppermute x1, waiting for transfers between devices: 8.47 us -> 3.5 us  [shards(): keep_h = move(own_h, perm=route['keep'])]
    ppermute x1, waiting for transfers between devices: 0.01 us -> 3.59 us  [shards(): keep_x = move(here_x, perm=route['relay'])]
    ppermute x1, starting transfers between devices: 0.01 us -> 3.27 us  [shards(): second_side = move(own_lists, perm=route['outer'])]
    ppermute x1, waiting for transfers between devices: 4.45 us -> 2.16 us  [shards(): turn_h = move(own_h, perm=route['turn'])]
    ppermute x1, starting transfers between devices: 0.1 us -> 1.49 us  [shards(): keep_x = move(keep_x, perm=route['relay'])]
  transfers between devices with their start and end apart: 20 -> 20, of which waited for: 9 -> 11; matrix products, arithmetic and copies ran while one was open for 2% -> 2% of each run, Pallas kernels for 5% -> 6%
where the time goes in v3:
time: 134 us
  waiting for transfers between devices  56.6 us (42%)
  starting transfers between devices  45.4 us (34%)
  Pallas kernels  24.2 us (18%)
  other arithmetic  3.95 us (3%)
  local copies, waits for them, and re-layouts  3.45 us (3%)
    ppermute x5, starting transfers between devices, shards(): outer = move(to_outer, perm=route['outer'])  28.7 us
    ppermute x5, waiting for transfers between devices, shards(): outer = move(to_outer, perm=route['outer'])  25 us
    pallas_call x4, Pallas kernels, run_orders(): pl.pallas_call(functools.partial(two_orders, order, last), out_shape=tupl...  16.8 us
    ppermute x1, waiting for transfers between devices, shards(): moved = move(moved, perm=route['turn_back'])  12.2 us
    ppermute x1, waiting for transfers between devices, shards(): kept = move(kept, perm=route['keep_back'])  5.59 us
    ppermute x1, waiting for transfers between devices, shards(): own_lists = move(neighbours, perm=route['turn'])  4.07 us
    ppermute x1, waiting for transfers between devices, shards(): keep_x = move(here_x, perm=route['relay'])  3.59 us
    ppermute x1, waiting for transfers between devices, shards(): keep_h = move(own_h, perm=route['keep'])  3.5 us
  transfers between devices with their start and end apart: 20, of which 11 were waited for; matrix products, arithmetic and copies ran while one was open for 2% of the time, Pallas kernels for 6%

profile of v3, /device:TPU:24, one launch (start us, length us, event | category | flops | bytes accessed | tf_op | source)
XLA Modules:
  0.0 133.8 jit_solution(5173518401725414035)
XLA Ops:
  1.6 4.1 %collective-permute-done.own = s32[6,4]{1,0:T(8,128)S(1)} collective-permute-done((s32[6,4]{1,0:T(8,128)S(1)}, s32[6,4]{1,0:T(8,128)S(1)}, u32[]{:S(2)}, u32[]{:S(2)}) %collective-permute-start) | collective-permute-done | bytes 128 | tf_op jit(solution)/shard_map/ppermute | solution.py:322
  5.6 1.9 %constant_dynamic-slice_fusion = (bf16[1,6,2,128,128]{4,3,2,1,0:T(8,128)(2,1)}, bf16[1,6,2,128,128]{4,3,2,1,0:T(8,128)(2,1)S(1)}) fusion(bf16[2,6,2,128,128]{4,3,2,1,0:T(8,128)(2,1)} %param.3, s32[]{:T(128)S(6)} %select_n.30, s32[]{:T(128)S(6)} %select_n.29), kind=kLoop, calls=%fused_computation.4 | loop fusion | bytes 1572872 | tf_op jit(solution)/shard_map/jit(dynamic_index_in_dim)/dynamic_slice | solution.py:329
  8.3 2.8 %collective-permute-start.3 = (bf16[12,128,128]{2,1,0:T(8,128)(2,1)S(1)}, bf16[12,128,128]{2,1,0:T(8,128)(2,1)S(1)}, u32[]{:S(2)}, u32[]{:S(2)}) collective-permute-start(bf16[12,128,128]{2,1,0:T(8,128)(2,1)S(1)} %bitcast.7), channel_id=1, source_target_pairs={{0,0},{1,5},{2,2},{3,7},{4,4},{5,1},{6,6},{7,3},{8,12},{9,9},{10,1... | collective-permute-start | bytes 1179656 | tf_op jit(solution)/shard_map/ppermute | solution.py:328
  11.2 2.6 %collective-permute-start.9 = (bf16[12,128,128]{2,1,0:T(8,128)(2,1)}, bf16[12,128,128]{2,1,0:T(8,128)(2,1)S(1)}, u32[]{:S(2)}, u32[]{:S(2)}) collective-permute-start(bf16[12,128,128]{2,1,0:T(8,128)(2,1)} %bitcast.2), channel_id=1, source_target_pairs={{0,5},{1,0},{2,7},{3,2},{4,1},{5,4},{6,3},{7,6},{8,9},{9,12},{10,1... | collective-permute-start | bytes 1179656 | tf_op jit(solution)/shard_map/ppermute | solution.py:332
  13.8 3.6 %collective-permute-done.7 = bf16[12,128,128]{2,1,0:T(8,128)(2,1)} collective-permute-done((bf16[12,128,128]{2,1,0:T(8,128)(2,1)S(1)}, bf16[12,128,128]{2,1,0:T(8,128)(2,1)}, u32[]{:S(2)}, u32[]{:S(2)}) %collective-permute-start.7) | collective-permute-done | bytes 393248 | tf_op jit(solution)/shard_map/ppermute | solution.py:331
  17.4 1.5 %collective-permute-start.8 = (bf16[12,128,128]{2,1,0:T(8,128)(2,1)}, bf16[12,128,128]{2,1,0:T(8,128)(2,1)S(1)}, u32[]{:S(2)}, u32[]{:S(2)}) collective-permute-start(bf16[12,128,128]{2,1,0:T(8,128)(2,1)} %collective-permute-done.7), channel_id=1, source_target_pairs={{0,1},{1,4},{2,3},{3,6},{4,5},{5,0},{6,7},{7,2},{8,13},{9,8},{10,1... | collective-permute-start | bytes 1179656 | tf_op jit(solution)/shard_map/ppermute | solution.py:333
  18.9 1.4 %make_pack.1.pack = s32[39]{0:T(128)} custom-call(s32[6,4]{1,0:T(8,128)} %copy-done.3), custom_call_target="tpu_custom_call" | custom-call | flops 1000000 | bytes 1024 | tf_op jit(solution)/shard_map/make_pack/pallas_call | solution.py:266
  20.3 3.5 %collective-permute-done.3.refs_0_ = bf16[12,128,128]{2,1,0:T(8,128)(2,1)S(1)} collective-permute-done((bf16[12,128,128]{2,1,0:T(8,128)(2,1)S(1)}, bf16[12,128,128]{2,1,0:T(8,128)(2,1)S(1)}, u32[]{:S(2)}, u32[]{:S(2)}) %collective-permute-start.3) | collective-permute-done | bytes 393248 | tf_op jit(solution)/shard_map/ppermute | solution.py:328
  23.8 3.3 %collective-permute-start.2 = (s32[6,4]{1,0:T(8,128)}, s32[6,4]{1,0:T(8,128)S(1)}, u32[]{:S(2)}, u32[]{:S(2)}) collective-permute-start(s32[6,4]{1,0:T(8,128)} %copy-done.3), channel_id=1, source_target_pairs={{0,250},{1,2},{2,1},{3,9},{4,7},{5,255},{6,12},{7,4},{8,11},{9,3},... | collective-permute-start | bytes 296 | tf_op jit(solution)/shard_map/ppermute | solution.py:326
  27.0 2.2 %collective-permute-done.4.refs_1_ = bf16[12,128,128]{2,1,0:T(8,128)(2,1)S(1)} collective-permute-done((bf16[12,128,128]{2,1,0:T(8,128)(2,1)S(1)}, bf16[12,128,128]{2,1,0:T(8,128)(2,1)S(1)}, u32[]{:S(2)}, u32[]{:S(2)}) %collective-permute-start.4) | collective-permute-done | bytes 393248 | tf_op jit(solution)/shard_map/ppermute | solution.py:327
  29.8 1.5 %assemble.2 = (bf16[24,128,128]{2,1,0:T(8,128)(2,1)S(1)}, bf16[18,128,128]{2,1,0:T(8,128)(2,1)S(1)}, bf16[18,128,128]{2,1,0:T(8,128)(2,1)}) custom-call(s32[39]{0:T(128)S(1)} %copy-done, bf16[12,128,128]{2,1,0:T(8,128)(2,1)S(1)} %collective-permute-done.3.refs_0_, bf16[12,128,128]{2,1,0:T(8,128)(2,1)S(1)} %collective-permute-done.4.refs_1_), custom_call_target="tpu_custom_call" | custom-call | bytes 3145728 | tf_op jit(solution)/shard_map/assemble/pallas_call | solution.py:289
  31.3 5.7 %collective-permute-start.6 = (bf16[18,128,128]{2,1,0:T(8,128)(2,1)}, bf16[18,128,128]{2,1,0:T(8,128)(2,1)}, u32[]{:S(2)}, u32[]{:S(2)}) collective-permute-start(bf16[18,128,128]{2,1,0:T(8,128)(2,1)} %get-tuple-element.36), channel_id=1, source_target_pairs={{0,250},{1,2},{2,1},{3,9},{4,7},{5,255},{6,12},{7,4},{8,11},{9,3},... | collective-permute-start | bytes 1769480 | tf_op jit(solution)/shard_map/ppermute | solution.py:341
  37.5 1.7 %assemble.3 = (bf16[24,128,128]{2,1,0:T(8,128)(2,1)S(1)}, bf16[18,128,128]{2,1,0:T(8,128)(2,1)}, bf16[18,128,128]{2,1,0:T(8,128)(2,1)}) custom-call(s32[39]{0:T(128)S(1)} %copy-done, bf16[12,128,128]{2,1,0:T(8,128)(2,1)S(1)} %bitcast.6, bf16[12,128,128]{2,1,0:T(8,128)(2,1)S(1)} %collective-permute-done.8.refs_1_, ...), custom_call_target="tpu_custom_call" | custom-call | bytes 3145728 | tf_op jit(solution)/shard_map/assemble/pallas_call | solution.py:289
  39.2 7.3 %collective-permute-start.11 = (bf16[18,128,128]{2,1,0:T(8,128)(2,1)}, bf16[18,128,128]{2,1,0:T(8,128)(2,1)}, u32[]{:S(2)}, u32[]{:S(2)}) collective-permute-start(bf16[18,128,128]{2,1,0:T(8,128)(2,1)} %get-tuple-element.40), channel_id=1, source_target_pairs={{0,250},{1,2},{2,1},{3,9},{4,7},{5,255},{6,12},{7,4},{8,11},{9,3},... | collective-permute-start | bytes 1769480 | tf_op jit(solution)/shard_map/ppermute | solution.py:350
  46.6 2.8 %make_table.1.table = s32[240]{0:T(256)} custom-call(s32[6,4]{1,0:T(8,128)} %copy-done.4, s32[6,4]{1,0:T(8,128)} %copy-done.3, s32[6,4]{1,0:T(8,128)} %copy-done.5), custom_call_target="tpu_custom_call" | custom-call | flops 1000000 | bytes 1024 | tf_op jit(solution)/shard_map/make_table/pallas_call | solution.py:277
  49.5 1.5 %maximum_maximum_fusion.operator = bf16[61,128,128]{2,1,0:T(8,128)(2,1)S(1)} fusion(bf16[18,128,128]{2,1,0:T(8,128)(2,1)} %collective-permute-done.6, bf16[24,128,128]{2,1,0:T(8,128)(2,1)S(1)} %get-tuple-element.35, bf16[18,128,128]{2,1,0:T(8,128)(2,1)} %collective-permute-done.5, bf16[61]{0:T(256)(128)(2,1)S(1)} %pad.3.clone), kind=kLoop, calls=%fused_computation | loop fusion | flops 2998272 | bytes 3965050 | tf_op jit(solution)/shard_map/concatenate | solution.py:344
  51.0 3.4 %collective-permute-done.11.outer = bf16[18,128,128]{2,1,0:T(8,128)(2,1)} collective-permute-done((bf16[18,128,128]{2,1,0:T(8,128)(2,1)}, bf16[18,128,128]{2,1,0:T(8,128)(2,1)}, u32[]{:S(2)}, u32[]{:S(2)}) %collective-permute-start.11) | collective-permute-done | bytes 589856 | tf_op jit(solution)/shard_map/ppermute | solution.py:350
  54.4 4.8 %two_orders.4 = (bf16[24,128,128]{2,1,0:T(8,128)(2,1)S(1)}, bf16[24,128,128]{2,1,0:T(8,128)(2,1)S(1)}, bf16[18,128,128]{2,1,0:T(8,128)(2,1)S(1)}, bf16[18,128,128]{2,1,0:T(8,128)(2,1)S(1)}) custom-call(s32[240]{0:T(256)S(1)} %copy-done.2, s32[39]{0:T(128)S(1)} %copy-done.1, bf16[61,128,128]{2,1,0:T(8,128)(2,1)S(1)} %maximum_maximum_fusion.operator, ...), custom_call_target="tpu_custom_call" | custom-call | flops 2415919104 | bytes 6291456 | tf_op jit(solution)/shard_map/two_orders/pallas_call | solution.py:302
  59.6 5.1 %collective-permute-start.13 = (bf16[18,128,128]{2,1,0:T(8,128)(2,1)S(1)}, bf16[18,128,128]{2,1,0:T(8,128)(2,1)S(1)}, u32[]{:S(2)}, u32[]{:S(2)}) collective-permute-start(bf16[18,128,128]{2,1,0:T(8,128)(2,1)S(1)} %get-tuple-element.43), channel_id=1, source_target_pairs={{0,250},{1,2},{2,1},{3,9},{4,7},{5,255},{6,12},{7,4},{8,11},{9,3},... | collective-permute-start | bytes 1769480 | tf_op jit(solution)/shard_map/ppermute | solution.py:350
  64.7 7.6 %collective-permute-done.13.outer = bf16[18,128,128]{2,1,0:T(8,128)(2,1)S(1)} collective-permute-done((bf16[18,128,128]{2,1,0:T(8,128)(2,1)S(1)}, bf16[18,128,128]{2,1,0:T(8,128)(2,1)S(1)}, u32[]{:S(2)}, u32[]{:S(2)}) %collective-permute-start.13) | collective-permute-done | bytes 589856 | tf_op jit(solution)/shard_map/ppermute | solution.py:350
  72.3 3.9 %two_orders.5 = (bf16[24,128,128]{2,1,0:T(8,128)(2,1)S(1)}, bf16[24,128,128]{2,1,0:T(8,128)(2,1)S(1)}, bf16[18,128,128]{2,1,0:T(8,128)(2,1)S(1)}, bf16[18,128,128]{2,1,0:T(8,128)(2,1)S(1)}) custom-call(s32[240]{0:T(256)S(1)} %copy-done.2, s32[39]{0:T(128)S(1)} %copy-done.1, bf16[61,128,128]{2,1,0:T(8,128)(2,1)S(1)} %maximum_maximum_fusion.operator, ...), custom_call_target="tpu_custom_call" | custom-call | flops 2415919104 | bytes 6291456 | tf_op jit(solution)/shard_map/two_orders/pallas_call | solution.py:302
  76.3 5.1 %collective-permute-start.15 = (bf16[18,128,128]{2,1,0:T(8,128)(2,1)S(1)}, bf16[18,128,128]{2,1,0:T(8,128)(2,1)S(1)}, u32[]{:S(2)}, u32[]{:S(2)}) collective-permute-start(bf16[18,128,128]{2,1,0:T(8,128)(2,1)S(1)} %get-tuple-element.46), channel_id=1, source_target_pairs={{0,250},{1,2},{2,1},{3,9},{4,7},{5,255},{6,12},{7,4},{8,11},{9,3},... | collective-permute-start | bytes 1769480 | tf_op jit(solution)/shard_map/ppermute | solution.py:350
  81.4 7.6 %collective-permute-done.15.outer = bf16[18,128,128]{2,1,0:T(8,128)(2,1)S(1)} collective-permute-done((bf16[18,128,128]{2,1,0:T(8,128)(2,1)S(1)}, bf16[18,128,128]{2,1,0:T(8,128)(2,1)S(1)}, u32[]{:S(2)}, u32[]{:S(2)}) %collective-permute-start.15) | collective-permute-done | bytes 589856 | tf_op jit(solution)/shard_map/ppermute | solution.py:350
  89.0 3.8 %two_orders.6 = (bf16[24,128,128]{2,1,0:T(8,128)(2,1)S(1)}, bf16[24,128,128]{2,1,0:T(8,128)(2,1)S(1)}, bf16[18,128,128]{2,1,0:T(8,128)(2,1)S(1)}, bf16[18,128,128]{2,1,0:T(8,128)(2,1)S(1)}) custom-call(s32[240]{0:T(256)S(1)} %copy-done.2, s32[39]{0:T(128)S(1)} %copy-done.1, bf16[61,128,128]{2,1,0:T(8,128)(2,1)S(1)} %maximum_maximum_fusion.operator, ...), custom_call_target="tpu_custom_call" | custom-call | flops 2415919104 | bytes 6291456 | tf_op jit(solution)/shard_map/two_orders/pallas_call | solution.py:302
  92.9 5.4 %collective-permute-start.17 = (bf16[18,128,128]{2,1,0:T(8,128)(2,1)S(1)}, bf16[18,128,128]{2,1,0:T(8,128)(2,1)S(1)}, u32[]{:S(2)}, u32[]{:S(2)}) collective-permute-start(bf16[18,128,128]{2,1,0:T(8,128)(2,1)S(1)} %get-tuple-element.49), channel_id=1, source_target_pairs={{0,250},{1,2},{2,1},{3,9},{4,7},{5,255},{6,12},{7,4},{8,11},{9,3},... | collective-permute-start | bytes 1769480 | tf_op jit(solution)/shard_map/ppermute | solution.py:350
  99.4 6.5 %collective-permute-done.17.outer = bf16[18,128,128]{2,1,0:T(8,128)(2,1)S(1)} collective-permute-done((bf16[18,128,128]{2,1,0:T(8,128)(2,1)S(1)}, bf16[18,128,128]{2,1,0:T(8,128)(2,1)S(1)}, u32[]{:S(2)}, u32[]{:S(2)}) %collective-permute-start.17) | collective-permute-done | bytes 589856 | tf_op jit(solution)/shard_map/ppermute | solution.py:350
  105.8 4.2 %two_orders.7 = (bf16[24,128,128]{2,1,0:T(8,128)(2,1)S(1)}, bf16[24,128,128]{2,1,0:T(8,128)(2,1)S(1)}) custom-call(s32[240]{0:T(256)S(1)} %copy-done.2, s32[39]{0:T(128)S(1)} %copy-done.1, bf16[61,128,128]{2,1,0:T(8,128)(2,1)S(1)} %maximum_maximum_fusion.operator, bf16[24,128,128]{2,1,0:T(8,128)(2,1)S(1)} %get-tuple-element.47.own, ...), custom_call_target="tpu_custom_call" | custom-call | flops 2415919104 | bytes 6291456 | tf_op jit(solution)/shard_map/two_orders/pallas_call | solution.py:302
  110.1 2.7 %collective-permute-start.19 = (bf16[24,128,128]{2,1,0:T(8,128)(2,1)S(1)}, bf16[24,128,128]{2,1,0:T(8,128)(2,1)S(1)}, u32[]{:S(2)}, u32[]{:S(2)}) collective-permute-start(bf16[24,128,128]{2,1,0:T(8,128)(2,1)S(1)} %get-tuple-element.54), channel_id=1, source_target_pairs={{0,1},{1,4},{2,3},{3,6},{4,5},{5,0},{6,7},{7,2},{8,13},{9,8},{10,1... | collective-permute-start | bytes 2359304 | tf_op jit(solution)/shard_map/ppermute | solution.py:363
  112.7 1.9 %collective-permute-start.18 = (bf16[24,128,128]{2,1,0:T(8,128)(2,1)S(1)}, bf16[24,128,128]{2,1,0:T(8,128)(2,1)S(1)}, u32[]{:S(2)}, u32[]{:S(2)}) collective-permute-start(bf16[24,128,128]{2,1,0:T(8,128)(2,1)S(1)} %get-tuple-element.53), channel_id=1, source_target_pairs={{0,0},{1,5},{2,2},{3,7},{4,4},{5,1},{6,6},{7,3},{8,12},{9,9},{10,1... | collective-permute-start | bytes 2359304 | tf_op jit(solution)/shard_map/ppermute | solution.py:362
  114.7 12.2 %collective-permute-done.19 = bf16[24,128,128]{2,1,0:T(8,128)(2,1)S(1)} collective-permute-done((bf16[24,128,128]{2,1,0:T(8,128)(2,1)S(1)}, bf16[24,128,128]{2,1,0:T(8,128)(2,1)S(1)}, u32[]{:S(2)}, u32[]{:S(2)}) %collective-permute-start.19) | collective-permute-done | bytes 786464 | tf_op jit(solution)/shard_map/ppermute | solution.py:363
  126.9 5.6 %collective-permute-done.18 = bf16[24,128,128]{2,1,0:T(8,128)(2,1)S(1)} collective-permute-done((bf16[24,128,128]{2,1,0:T(8,128)(2,1)S(1)}, bf16[24,128,128]{2,1,0:T(8,128)(2,1)S(1)}, u32[]{:S(2)}, u32[]{:S(2)}) %collective-permute-start.18) | collective-permute-done | bytes 786464 | tf_op jit(solution)/shard_map/ppermute | solution.py:362
  132.5 1.4 %convert_add_fusion = f32[24,128,128]{2,1,0:T(8,128)} fusion(bf16[24,128,128]{2,1,0:T(8,128)(2,1)S(1)} %collective-permute-done.19, bf16[24,128,128]{2,1,0:T(8,128)(2,1)S(1)} %collective-permute-done.18), kind=kLoop, calls=%fused_computation.1 | loop fusion | flops 1179648 | bytes 3145728 | tf_op jit(solution)/shard_map/add | solution.py:364
  (36 shorter events, 5.2 us)
Async XLA Ops:
  0.0 8.3 %copy-start.6 = (bf16[6,2,128,128]{3,2,1,0:T(8,128)(2,1)S(1)}, bf16[6,2,128,128]{3,2,1,0:T(8,128)(2,1)}, u32[]{:S(2)}) copy-start(bf16[6,2,128,128]{3,2,1,0:T(8,128)(2,1)} %param.4) | copy-start | bytes 1179652
  0.8 4.8 %collective-permute-start = (s32[6,4]{1,0:T(8,128)S(1)}, s32[6,4]{1,0:T(8,128)S(1)}, u32[]{:S(2)}, u32[]{:S(2)}) collective-permute-start(s32[6,4]{1,0:T(8,128)S(1)} %copy.4), channel_id=1, source_target_pairs={{0,5},{1,0},{2,7},{3,2},{4,1},{5,4},{6,3},{7,6},{8,9},{9,12},{10,1... | collective-permute-start | bytes 296 | tf_op jit(solution)/shard_map/ppermute | solution.py:322
  5.6 13.2 %copy-start.3 = (s32[6,4]{1,0:T(8,128)}, s32[6,4]{1,0:T(8,128)S(1)}, u32[]{:S(2)}) copy-start(s32[6,4]{1,0:T(8,128)S(1)} %collective-permute-done.own) | copy-start | bytes 292
  7.6 9.8 %collective-permute-start.7 = (bf16[12,128,128]{2,1,0:T(8,128)(2,1)S(1)}, bf16[12,128,128]{2,1,0:T(8,128)(2,1)}, u32[]{:S(2)}, u32[]{:S(2)}) collective-permute-start(bf16[12,128,128]{2,1,0:T(8,128)(2,1)S(1)} %bitcast.5), channel_id=1, source_target_pairs={{0,1},{1,4},{2,3},{3,6},{4,5},{5,0},{6,7},{7,2},{8,13},{9,8},{10,1... | collective-permute-start | bytes 1179656 | tf_op jit(solution)/shard_map/ppermute | solution.py:331
  8.3 15.4 %collective-permute-start.3 = (bf16[12,128,128]{2,1,0:T(8,128)(2,1)S(1)}, bf16[12,128,128]{2,1,0:T(8,128)(2,1)S(1)}, u32[]{:S(2)}, u32[]{:S(2)}) collective-permute-start(bf16[12,128,128]{2,1,0:T(8,128)(2,1)S(1)} %bitcast.7), channel_id=1, source_target_pairs={{0,0},{1,5},{2,2},{3,7},{4,4},{5,1},{6,6},{7,3},{8,12},{9,9},{10,1... | collective-permute-start | bytes 1179656 | tf_op jit(solution)/shard_map/ppermute | solution.py:328
  11.1 18.1 %collective-permute-start.4 = (bf16[12,128,128]{2,1,0:T(8,128)(2,1)S(1)}, bf16[12,128,128]{2,1,0:T(8,128)(2,1)S(1)}, u32[]{:S(2)}, u32[]{:S(2)}) collective-permute-start(bf16[12,128,128]{2,1,0:T(8,128)(2,1)S(1)} %bitcast.8), channel_id=1, source_target_pairs={{0,5},{1,0},{2,7},{3,2},{4,1},{5,4},{6,3},{7,6},{8,9},{9,12},{10,1... | collective-permute-start | bytes 1179656 | tf_op jit(solution)/shard_map/ppermute | solution.py:327
  11.2 26.4 %collective-permute-start.9 = (bf16[12,128,128]{2,1,0:T(8,128)(2,1)}, bf16[12,128,128]{2,1,0:T(8,128)(2,1)S(1)}, u32[]{:S(2)}, u32[]{:S(2)}) collective-permute-start(bf16[12,128,128]{2,1,0:T(8,128)(2,1)} %bitcast.2), channel_id=1, source_target_pairs={{0,5},{1,0},{2,7},{3,2},{4,1},{5,4},{6,3},{7,6},{8,9},{9,12},{10,1... | collective-permute-start | bytes 1179656 | tf_op jit(solution)/shard_map/ppermute | solution.py:332
  17.4 20.1 %collective-permute-start.8 = (bf16[12,128,128]{2,1,0:T(8,128)(2,1)}, bf16[12,128,128]{2,1,0:T(8,128)(2,1)S(1)}, u32[]{:S(2)}, u32[]{:S(2)}) collective-permute-start(bf16[12,128,128]{2,1,0:T(8,128)(2,1)} %collective-permute-done.7), channel_id=1, source_target_pairs={{0,1},{1,4},{2,3},{3,6},{4,5},{5,0},{6,7},{7,2},{8,13},{9,8},{10,1... | collective-permute-start | bytes 1179656 | tf_op jit(solution)/shard_map/ppermute | solution.py:333
  18.9 12.4 %collective-permute-start.1 = (s32[6,4]{1,0:T(8,128)S(1)}, s32[6,4]{1,0:T(8,128)S(1)}, u32[]{:S(2)}, u32[]{:S(2)}) collective-permute-start(s32[6,4]{1,0:T(8,128)S(1)} %collective-permute-done.own), channel_id=1, source_target_pairs={{0,2},{1,3},{2,0},{3,1},{4,6},{5,7},{6,4},{7,5},{8,10},{9,11},{10,... | collective-permute-start | bytes 296 | tf_op jit(solution)/shard_map/ppermute | solution.py:325
  23.8 7.5 %collective-permute-start.2 = (s32[6,4]{1,0:T(8,128)}, s32[6,4]{1,0:T(8,128)S(1)}, u32[]{:S(2)}, u32[]{:S(2)}) collective-permute-start(s32[6,4]{1,0:T(8,128)} %copy-done.3), channel_id=1, source_target_pairs={{0,250},{1,2},{2,1},{3,9},{4,7},{5,255},{6,12},{7,4},{8,11},{9,3},... | collective-permute-start | bytes 296 | tf_op jit(solution)/shard_map/ppermute | solution.py:326
  29.2 0.6 copy-start
  31.3 15.3 %copy-start.4 = (s32[6,4]{1,0:T(8,128)}, s32[6,4]{1,0:T(8,128)S(1)}, u32[]{:S(2)}) copy-start(s32[6,4]{1,0:T(8,128)S(1)} %collective-permute-done.1.inner) | copy-start | bytes 292
  31.3 15.3 %copy-start.5 = (s32[6,4]{1,0:T(8,128)}, s32[6,4]{1,0:T(8,128)S(1)}, u32[]{:S(2)}) copy-start(s32[6,4]{1,0:T(8,128)S(1)} %collective-permute-done.2.outer) | copy-start | bytes 292
  31.3 18.2 %collective-permute-start.6 = (bf16[18,128,128]{2,1,0:T(8,128)(2,1)}, bf16[18,128,128]{2,1,0:T(8,128)(2,1)}, u32[]{:S(2)}, u32[]{:S(2)}) collective-permute-start(bf16[18,128,128]{2,1,0:T(8,128)(2,1)} %get-tuple-element.36), channel_id=1, source_target_pairs={{0,250},{1,2},{2,1},{3,9},{4,7},{5,255},{6,12},{7,4},{8,11},{9,3},... | collective-permute-start | bytes 1769480 | tf_op jit(solution)/shard_map/ppermute | solution.py:341
  37.0 12.5 %collective-permute-start.5 = (bf16[18,128,128]{2,1,0:T(8,128)(2,1)S(1)}, bf16[18,128,128]{2,1,0:T(8,128)(2,1)}, u32[]{:S(2)}, u32[]{:S(2)}) collective-permute-start(bf16[18,128,128]{2,1,0:T(8,128)(2,1)S(1)} %get-tuple-element.34), channel_id=1, source_target_pairs={{0,2},{1,3},{2,0},{3,1},{4,6},{5,7},{6,4},{7,5},{8,10},{9,11},{10,... | collective-permute-start | bytes 1769480 | tf_op jit(solution)/shard_map/ppermute | solution.py:342
  39.2 11.8 %collective-permute-start.10 = (bf16[18,128,128]{2,1,0:T(8,128)(2,1)}, bf16[18,128,128]{2,1,0:T(8,128)(2,1)S(1)}, u32[]{:S(2)}, u32[]{:S(2)}) collective-permute-start(bf16[18,128,128]{2,1,0:T(8,128)(2,1)} %get-tuple-element.39), channel_id=1, source_target_pairs={{0,2},{1,3},{2,0},{3,1},{4,6},{5,7},{6,4},{7,5},{8,10},{9,11},{10,... | collective-permute-start | bytes 1769480 | tf_op jit(solution)/shard_map/ppermute | solution.py:351
  39.2 15.2 %collective-permute-start.11 = (bf16[18,128,128]{2,1,0:T(8,128)(2,1)}, bf16[18,128,128]{2,1,0:T(8,128)(2,1)}, u32[]{:S(2)}, u32[]{:S(2)}) collective-permute-start(bf16[18,128,128]{2,1,0:T(8,128)(2,1)} %get-tuple-element.40), channel_id=1, source_target_pairs={{0,250},{1,2},{2,1},{3,9},{4,7},{5,255},{6,12},{7,4},{8,11},{9,3},... | collective-permute-start | bytes 1769480 | tf_op jit(solution)/shard_map/ppermute | solution.py:350
  49.5 4.9 %copy-start.1 = (s32[39]{0:T(128)S(1)}, s32[39]{0:T(128)}, u32[]{:S(2)}) copy-start(s32[39]{0:T(128)} %make_pack.1.pack) | copy-start | bytes 472
  49.5 4.9 %copy-start.2 = (s32[240]{0:T(256)S(1)}, s32[240]{0:T(256)}, u32[]{:S(2)}) copy-start(s32[240]{0:T(256)} %make_table.1.table) | copy-start | bytes 2884
  59.3 5.4 %collective-permute-start.12 = (bf16[18,128,128]{2,1,0:T(8,128)(2,1)S(1)}, bf16[18,128,128]{2,1,0:T(8,128)(2,1)S(1)}, u32[]{:S(2)}, u32[]{:S(2)}) collective-permute-start(bf16[18,128,128]{2,1,0:T(8,128)(2,1)S(1)} %get-tuple-element.42), channel_id=1, source_target_pairs={{0,2},{1,3},{2,0},{3,1},{4,6},{5,7},{6,4},{7,5},{8,10},{9,11},{10,... | collective-permute-start | bytes 1769480 | tf_op jit(solution)/shard_map/ppermute | solution.py:351
  59.6 12.7 %collective-permute-start.13 = (bf16[18,128,128]{2,1,0:T(8,128)(2,1)S(1)}, bf16[18,128,128]{2,1,0:T(8,128)(2,1)S(1)}, u32[]{:S(2)}, u32[]{:S(2)}) collective-permute-start(bf16[18,128,128]{2,1,0:T(8,128)(2,1)S(1)} %get-tuple-element.43), channel_id=1, source_target_pairs={{0,250},{1,2},{2,1},{3,9},{4,7},{5,255},{6,12},{7,4},{8,11},{9,3},... | collective-permute-start | bytes 1769480 | tf_op jit(solution)/shard_map/ppermute | solution.py:350
  76.2 5.2 %collective-permute-start.14 = (bf16[18,128,128]{2,1,0:T(8,128)(2,1)S(1)}, bf16[18,128,128]{2,1,0:T(8,128)(2,1)S(1)}, u32[]{:S(2)}, u32[]{:S(2)}) collective-permute-start(bf16[18,128,128]{2,1,0:T(8,128)(2,1)S(1)} %get-tuple-element.45), channel_id=1, source_target_pairs={{0,2},{1,3},{2,0},{3,1},{4,6},{5,7},{6,4},{7,5},{8,10},{9,11},{10,... | collective-permute-start | bytes 1769480 | tf_op jit(solution)/shard_map/ppermute | solution.py:351
  76.3 12.7 %collective-permute-start.15 = (bf16[18,128,128]{2,1,0:T(8,128)(2,1)S(1)}, bf16[18,128,128]{2,1,0:T(8,128)(2,1)S(1)}, u32[]{:S(2)}, u32[]{:S(2)}) collective-permute-start(bf16[18,128,128]{2,1,0:T(8,128)(2,1)S(1)} %get-tuple-element.46), channel_id=1, source_target_pairs={{0,250},{1,2},{2,1},{3,9},{4,7},{5,255},{6,12},{7,4},{8,11},{9,3},... | collective-permute-start | bytes 1769480 | tf_op jit(solution)/shard_map/ppermute | solution.py:350
  92.8 6.5 %collective-permute-start.16 = (bf16[18,128,128]{2,1,0:T(8,128)(2,1)S(1)}, bf16[18,128,128]{2,1,0:T(8,128)(2,1)S(1)}, u32[]{:S(2)}, u32[]{:S(2)}) collective-permute-start(bf16[18,128,128]{2,1,0:T(8,128)(2,1)S(1)} %get-tuple-element.48), channel_id=1, source_target_pairs={{0,2},{1,3},{2,0},{3,1},{4,6},{5,7},{6,4},{7,5},{8,10},{9,11},{10,... | collective-permute-start | bytes 1769480 | tf_op jit(solution)/shard_map/ppermute | solution.py:351
  92.9 12.9 %collective-permute-start.17 = (bf16[18,128,128]{2,1,0:T(8,128)(2,1)S(1)}, bf16[18,128,128]{2,1,0:T(8,128)(2,1)S(1)}, u32[]{:S(2)}, u32[]{:S(2)}) collective-permute-start(bf16[18,128,128]{2,1,0:T(8,128)(2,1)S(1)} %get-tuple-element.49), channel_id=1, source_target_pairs={{0,250},{1,2},{2,1},{3,9},{4,7},{5,255},{6,12},{7,4},{8,11},{9,3},... | collective-permute-start | bytes 1769480 | tf_op jit(solution)/shard_map/ppermute | solution.py:350
  110.1 16.8 %collective-permute-start.19 = (bf16[24,128,128]{2,1,0:T(8,128)(2,1)S(1)}, bf16[24,128,128]{2,1,0:T(8,128)(2,1)S(1)}, u32[]{:S(2)}, u32[]{:S(2)}) collective-permute-start(bf16[24,128,128]{2,1,0:T(8,128)(2,1)S(1)} %get-tuple-element.54), channel_id=1, source_target_pairs={{0,1},{1,4},{2,3},{3,6},{4,5},{5,0},{6,7},{7,2},{8,13},{9,8},{10,1... | collective-permute-start | bytes 2359304 | tf_op jit(solution)/shard_map/ppermute | solution.py:363
  112.7 19.7 %collective-permute-start.18 = (bf16[24,128,128]{2,1,0:T(8,128)(2,1)S(1)}, bf16[24,128,128]{2,1,0:T(8,128)(2,1)S(1)}, u32[]{:S(2)}, u32[]{:S(2)}) collective-permute-start(bf16[24,128,128]{2,1,0:T(8,128)(2,1)S(1)} %get-tuple-element.53), channel_id=1, source_target_pairs={{0,0},{1,5},{2,2},{3,7},{4,4},{5,1},{6,6},{7,3},{8,12},{9,9},{10,1... | collective-permute-start | bytes 2359304 | tf_op jit(solution)/shard_map/ppermute | solution.py:362

commit v4 on v3

--- a/solution.py
+++ b/solution.py
@@ -335,15 +335,16 @@
     pack = run_pack(own_lists)
     operator, to_inner, to_outer = run_assemble(False, pack, keep_h, turn_h)
     table = run_table(first_side, own_lists, second_side)
-    to_inner, to_outer, first_side, second_side = lax.optimization_barrier(
-        (to_inner, to_outer, first_side, second_side)
+    term, term_inner, term_outer = run_assemble(True, pack, here_x, keep_x, turn_x)
+    to_inner, to_outer, term_inner, term_outer, first_side, second_side = lax.optimization_barrier(
+        (to_inner, to_outer, term_inner, term_outer, first_side, second_side)
     )
     outer = move(to_outer, perm=route["outer"])
     inner = move(to_inner, perm=route["inner"])
     zero = jnp.zeros((1, BLOCK, BLOCK), jnp.bfloat16)
     operator = jnp.concatenate([inner, operator, outer, zero], axis=0)
 
-    term, to_inner, to_outer = run_assemble(True, pack, here_x, keep_x, turn_x)
+    to_inner, to_outer = term_inner, term_outer
     sums = [term.astype(jnp.float32) * WEIGHT[0], jnp.zeros((), jnp.float32)]
     count = STEPS * ORDERS
     for order in range(1, count, 2):

time: 134 us -> 140 us (1.045)
  waiting for transfers between devices: 56.6 us -> 67.1 us
  starting transfers between devices: 45.4 us -> 41 us
    ppermute x5, starting transfers between devices: 28.7 us -> 22.7 us  [shards(): outer = move(to_outer, perm=route['outer'])]
    ppermute x1, waiting for transfers between devices: 0.5 us -> 6.24 us  [shards(): turn_x = move(turn_x, perm=route['turn'])]
    ppermute x5, waiting for transfers between devices: 25 us -> 29.7 us  [shards(): outer = move(to_outer, perm=route['outer'])]
  transfers between devices with their start and end apart: 20 -> 20, of which waited for: 11 -> 12; matrix products, arithmetic and copies ran while one was open for 2% -> 2% of each run, Pallas kernels for 6% -> 5%
where the time goes in v4:
time: 140 us
  waiting for transfers between devices  67.1 us (48%)
  starting transfers between devices  41 us (29%)
  Pallas kernels  24.2 us (17%)
  other arithmetic  3.95 us (3%)
  local copies, waits for them, and re-layouts  3.45 us (2%)
    ppermute x5, waiting for transfers between devices, shards(): outer = move(to_outer, perm=route['outer'])  29.7 us
    ppermute x5, starting transfers between devices, shards(): outer = move(to_outer, perm=route['outer'])  22.7 us
    pallas_call x4, Pallas kernels, run_orders(): pl.pallas_call(functools.partial(two_orders, order, last), out_shape=tupl...  16.8 us
    ppermute x1, waiting for transfers between devices, shards(): moved = move(moved, perm=route['turn_back'])  12.2 us
    ppermute x1, waiting for transfers between devices, shards(): turn_x = move(turn_x, perm=route['turn'])  6.24 us
    ppermute x1, waiting for transfers between devices, shards(): kept = move(kept, perm=route['keep_back'])  5.59 us
    ppermute x1, waiting for transfers between devices, shards(): own_lists = move(neighbours, perm=route['turn'])  4.07 us
    ppermute x1, starting transfers between devices, shards(): moved = move(moved, perm=route['turn_back'])  3.66 us
  transfers between devices with their start and end apart: 20, of which 12 were waited for; matrix products, arithmetic and copies ran while one was open for 2% of the time, Pallas kernels for 5%

profile of v4, /device:TPU:24, one launch (start us, length us, event | category | flops | bytes accessed | tf_op | source)
XLA Modules:
  0.0 139.8 jit_solution(7264212995066012518)
XLA Ops:
  1.6 4.1 %collective-permute-done.own = s32[6,4]{1,0:T(8,128)S(1)} collective-permute-done((s32[6,4]{1,0:T(8,128)S(1)}, s32[6,4]{1,0:T(8,128)S(1)}, u32[]{:S(2)}, u32[]{:S(2)}) %collective-permute-start) | collective-permute-done | bytes 128 | tf_op jit(solution)/shard_map/ppermute | solution.py:322
  5.6 1.9 %constant_dynamic-slice_fusion = (bf16[1,6,2,128,128]{4,3,2,1,0:T(8,128)(2,1)}, bf16[1,6,2,128,128]{4,3,2,1,0:T(8,128)(2,1)S(1)}) fusion(bf16[2,6,2,128,128]{4,3,2,1,0:T(8,128)(2,1)} %param.3, s32[]{:T(128)S(6)} %select_n.30, s32[]{:T(128)S(6)} %select_n.29), kind=kLoop, calls=%fused_computation.4 | loop fusion | bytes 1572872 | tf_op jit(solution)/shard_map/jit(dynamic_index_in_dim)/dynamic_slice | solution.py:329
  8.3 2.8 %collective-permute-start.3 = (bf16[12,128,128]{2,1,0:T(8,128)(2,1)S(1)}, bf16[12,128,128]{2,1,0:T(8,128)(2,1)S(1)}, u32[]{:S(2)}, u32[]{:S(2)}) collective-permute-start(bf16[12,128,128]{2,1,0:T(8,128)(2,1)S(1)} %bitcast.7), channel_id=1, source_target_pairs={{0,0},{1,5},{2,2},{3,7},{4,4},{5,1},{6,6},{7,3},{8,12},{9,9},{10,1... | collective-permute-start | bytes 1179656 | tf_op jit(solution)/shard_map/ppermute | solution.py:328
  11.2 2.6 %collective-permute-start.7 = (bf16[12,128,128]{2,1,0:T(8,128)(2,1)}, bf16[12,128,128]{2,1,0:T(8,128)(2,1)S(1)}, u32[]{:S(2)}, u32[]{:S(2)}) collective-permute-start(bf16[12,128,128]{2,1,0:T(8,128)(2,1)} %bitcast.2), channel_id=1, source_target_pairs={{0,5},{1,0},{2,7},{3,2},{4,1},{5,4},{6,3},{7,6},{8,9},{9,12},{10,1... | collective-permute-start | bytes 1179656 | tf_op jit(solution)/shard_map/ppermute | solution.py:332
  13.8 3.6 %collective-permute-done.5 = bf16[12,128,128]{2,1,0:T(8,128)(2,1)} collective-permute-done((bf16[12,128,128]{2,1,0:T(8,128)(2,1)S(1)}, bf16[12,128,128]{2,1,0:T(8,128)(2,1)}, u32[]{:S(2)}, u32[]{:S(2)}) %collective-permute-start.5) | collective-permute-done | bytes 393248 | tf_op jit(solution)/shard_map/ppermute | solution.py:331
  17.4 1.5 %collective-permute-start.6 = (bf16[12,128,128]{2,1,0:T(8,128)(2,1)}, bf16[12,128,128]{2,1,0:T(8,128)(2,1)S(1)}, u32[]{:S(2)}, u32[]{:S(2)}) collective-permute-start(bf16[12,128,128]{2,1,0:T(8,128)(2,1)} %collective-permute-done.5), channel_id=1, source_target_pairs={{0,1},{1,4},{2,3},{3,6},{4,5},{5,0},{6,7},{7,2},{8,13},{9,8},{10,1... | collective-permute-start | bytes 1179656 | tf_op jit(solution)/shard_map/ppermute | solution.py:333
  18.9 1.4 make_pack.1.pack
  20.3 3.5 %collective-permute-done.3.refs_0_ = bf16[12,128,128]{2,1,0:T(8,128)(2,1)S(1)} collective-permute-done((bf16[12,128,128]{2,1,0:T(8,128)(2,1)S(1)}, bf16[12,128,128]{2,1,0:T(8,128)(2,1)S(1)}, u32[]{:S(2)}, u32[]{:S(2)}) %collective-permute-start.3) | collective-permute-done | bytes 393248 | tf_op jit(solution)/shard_map/ppermute | solution.py:328
  23.8 3.3 %collective-permute-start.2 = (s32[6,4]{1,0:T(8,128)}, s32[6,4]{1,0:T(8,128)S(1)}, u32[]{:S(2)}, u32[]{:S(2)}) collective-permute-start(s32[6,4]{1,0:T(8,128)} %copy-done.3), channel_id=1, source_target_pairs={{0,250},{1,2},{2,1},{3,9},{4,7},{5,255},{6,12},{7,4},{8,11},{9,3},... | collective-permute-start | bytes 296 | tf_op jit(solution)/shard_map/ppermute | solution.py:326
  27.0 2.2 %collective-permute-done.4.refs_1_ = bf16[12,128,128]{2,1,0:T(8,128)(2,1)S(1)} collective-permute-done((bf16[12,128,128]{2,1,0:T(8,128)(2,1)S(1)}, bf16[12,128,128]{2,1,0:T(8,128)(2,1)S(1)}, u32[]{:S(2)}, u32[]{:S(2)}) %collective-permute-start.4) | collective-permute-done | bytes 393248 | tf_op jit(solution)/shard_map/ppermute | solution.py:327
  29.8 1.5 %assemble.2 = (bf16[24,128,128]{2,1,0:T(8,128)(2,1)S(1)}, bf16[18,128,128]{2,1,0:T(8,128)(2,1)S(1)}, bf16[18,128,128]{2,1,0:T(8,128)(2,1)}) custom-call(s32[39]{0:T(128)S(1)} %copy-done, bf16[12,128,128]{2,1,0:T(8,128)(2,1)S(1)} %collective-permute-done.3.refs_0_, bf16[12,128,128]{2,1,0:T(8,128)(2,1)S(1)} %collective-permute-done.4.refs_1_), custom_call_target="tpu_custom_call" | custom-call | bytes 3145728 | tf_op jit(solution)/shard_map/assemble/pallas_call | solution.py:289
  31.3 6.2 %collective-permute-done.7.refs_2_ = bf16[12,128,128]{2,1,0:T(8,128)(2,1)S(1)} collective-permute-done((bf16[12,128,128]{2,1,0:T(8,128)(2,1)}, bf16[12,128,128]{2,1,0:T(8,128)(2,1)S(1)}, u32[]{:S(2)}, u32[]{:S(2)}) %collective-permute-start.7) | collective-permute-done | bytes 393248 | tf_op jit(solution)/shard_map/ppermute | solution.py:332
  37.5 1.7 %assemble.3 = (bf16[24,128,128]{2,1,0:T(8,128)(2,1)S(1)}, bf16[18,128,128]{2,1,0:T(8,128)(2,1)}, bf16[18,128,128]{2,1,0:T(8,128)(2,1)}) custom-call(s32[39]{0:T(128)S(1)} %copy-done, bf16[12,128,128]{2,1,0:T(8,128)(2,1)S(1)} %bitcast.6, bf16[12,128,128]{2,1,0:T(8,128)(2,1)S(1)} %collective-permute-done.6.refs_1_, ...), custom_call_target="tpu_custom_call" | custom-call | bytes 3145728 | tf_op jit(solution)/shard_map/assemble/pallas_call | solution.py:289
  39.3 5.9 %collective-permute-start.9 = (bf16[18,128,128]{2,1,0:T(8,128)(2,1)}, bf16[18,128,128]{2,1,0:T(8,128)(2,1)}, u32[]{:S(2)}, u32[]{:S(2)}) collective-permute-start(bf16[18,128,128]{2,1,0:T(8,128)(2,1)} %get-tuple-element.41), channel_id=1, source_target_pairs={{0,250},{1,2},{2,1},{3,9},{4,7},{5,255},{6,12},{7,4},{8,11},{9,3},... | collective-permute-start | bytes 1769480 | tf_op jit(solution)/shard_map/ppermute | solution.py:342
  47.0 2.8 %make_table.1.table = s32[240]{0:T(256)} custom-call(s32[6,4]{1,0:T(8,128)} %copy-done.4, s32[6,4]{1,0:T(8,128)} %copy-done.3, s32[6,4]{1,0:T(8,128)} %copy-done.5), custom_call_target="tpu_custom_call" | custom-call | flops 1000000 | bytes 1024 | tf_op jit(solution)/shard_map/make_table/pallas_call | solution.py:277
  49.8 3.3 %collective-permute-done.9 = bf16[18,128,128]{2,1,0:T(8,128)(2,1)} collective-permute-done((bf16[18,128,128]{2,1,0:T(8,128)(2,1)}, bf16[18,128,128]{2,1,0:T(8,128)(2,1)}, u32[]{:S(2)}, u32[]{:S(2)}) %collective-permute-start.9) | collective-permute-done | bytes 589856 | tf_op jit(solution)/shard_map/ppermute | solution.py:342
  53.1 1.5 %maximum_maximum_fusion.operator = bf16[61,128,128]{2,1,0:T(8,128)(2,1)S(1)} fusion(bf16[18,128,128]{2,1,0:T(8,128)(2,1)} %collective-permute-done.9, bf16[24,128,128]{2,1,0:T(8,128)(2,1)S(1)} %get-tuple-element.40, bf16[18,128,128]{2,1,0:T(8,128)(2,1)} %collective-permute-done.8, bf16[61]{0:T(256)(128)(2,1)S(1)} %pad.3.clone), kind=kLoop, calls=%fused_computation | loop fusion | flops 2998272 | bytes 3965050 | tf_op jit(solution)/shard_map/concatenate | solution.py:345
  54.6 4.8 %collective-permute-done.11.outer = bf16[18,128,128]{2,1,0:T(8,128)(2,1)} collective-permute-done((bf16[18,128,128]{2,1,0:T(8,128)(2,1)}, bf16[18,128,128]{2,1,0:T(8,128)(2,1)}, u32[]{:S(2)}, u32[]{:S(2)}) %collective-permute-start.11) | collective-permute-done | bytes 589856 | tf_op jit(solution)/shard_map/ppermute | solution.py:351
  59.4 4.8 %two_orders.4 = (bf16[24,128,128]{2,1,0:T(8,128)(2,1)S(1)}, bf16[24,128,128]{2,1,0:T(8,128)(2,1)S(1)}, bf16[18,128,128]{2,1,0:T(8,128)(2,1)S(1)}, bf16[18,128,128]{2,1,0:T(8,128)(2,1)S(1)}) custom-call(s32[240]{0:T(256)S(1)} %copy-done.2, s32[39]{0:T(128)S(1)} %copy-done.1, bf16[61,128,128]{2,1,0:T(8,128)(2,1)S(1)} %maximum_maximum_fusion.operator, ...), custom_call_target="tpu_custom_call" | custom-call | flops 2415919104 | bytes 6291456 | tf_op jit(solution)/shard_map/two_orders/pallas_call | solution.py:302
  64.5 5.1 %collective-permute-start.13 = (bf16[18,128,128]{2,1,0:T(8,128)(2,1)S(1)}, bf16[18,128,128]{2,1,0:T(8,128)(2,1)S(1)}, u32[]{:S(2)}, u32[]{:S(2)}) collective-permute-start(bf16[18,128,128]{2,1,0:T(8,128)(2,1)S(1)} %get-tuple-element.47), channel_id=1, source_target_pairs={{0,250},{1,2},{2,1},{3,9},{4,7},{5,255},{6,12},{7,4},{8,11},{9,3},... | collective-permute-start | bytes 1769480 | tf_op jit(solution)/shard_map/ppermute | solution.py:351
  69.6 7.6 %collective-permute-done.13.outer = bf16[18,128,128]{2,1,0:T(8,128)(2,1)S(1)} collective-permute-done((bf16[18,128,128]{2,1,0:T(8,128)(2,1)S(1)}, bf16[18,128,128]{2,1,0:T(8,128)(2,1)S(1)}, u32[]{:S(2)}, u32[]{:S(2)}) %collective-permute-start.13) | collective-permute-done | bytes 589856 | tf_op jit(solution)/shard_map/ppermute | solution.py:351
  77.2 3.9 %two_orders.5 = (bf16[24,128,128]{2,1,0:T(8,128)(2,1)S(1)}, bf16[24,128,128]{2,1,0:T(8,128)(2,1)S(1)}, bf16[18,128,128]{2,1,0:T(8,128)(2,1)S(1)}, bf16[18,128,128]{2,1,0:T(8,128)(2,1)S(1)}) custom-call(s32[240]{0:T(256)S(1)} %copy-done.2, s32[39]{0:T(128)S(1)} %copy-done.1, bf16[61,128,128]{2,1,0:T(8,128)(2,1)S(1)} %maximum_maximum_fusion.operator, ...), custom_call_target="tpu_custom_call" | custom-call | flops 2415919104 | bytes 6291456 | tf_op jit(solution)/shard_map/two_orders/pallas_call | solution.py:302
  81.2 5.1 %collective-permute-start.15 = (bf16[18,128,128]{2,1,0:T(8,128)(2,1)S(1)}, bf16[18,128,128]{2,1,0:T(8,128)(2,1)S(1)}, u32[]{:S(2)}, u32[]{:S(2)}) collective-permute-start(bf16[18,128,128]{2,1,0:T(8,128)(2,1)S(1)} %get-tuple-element.50), channel_id=1, source_target_pairs={{0,250},{1,2},{2,1},{3,9},{4,7},{5,255},{6,12},{7,4},{8,11},{9,3},... | collective-permute-start | bytes 1769480 | tf_op jit(solution)/shard_map/ppermute | solution.py:351
  86.4 7.6 %collective-permute-done.15.outer = bf16[18,128,128]{2,1,0:T(8,128)(2,1)S(1)} collective-permute-done((bf16[18,128,128]{2,1,0:T(8,128)(2,1)S(1)}, bf16[18,128,128]{2,1,0:T(8,128)(2,1)S(1)}, u32[]{:S(2)}, u32[]{:S(2)}) %collective-permute-start.15) | collective-permute-done | bytes 589856 | tf_op jit(solution)/shard_map/ppermute | solution.py:351
  94.0 3.8 %two_orders.6 = (bf16[24,128,128]{2,1,0:T(8,128)(2,1)S(1)}, bf16[24,128,128]{2,1,0:T(8,128)(2,1)S(1)}, bf16[18,128,128]{2,1,0:T(8,128)(2,1)S(1)}, bf16[18,128,128]{2,1,0:T(8,128)(2,1)S(1)}) custom-call(s32[240]{0:T(256)S(1)} %copy-done.2, s32[39]{0:T(128)S(1)} %copy-done.1, bf16[61,128,128]{2,1,0:T(8,128)(2,1)S(1)} %maximum_maximum_fusion.operator, ...), custom_call_target="tpu_custom_call" | custom-call | flops 2415919104 | bytes 6291456 | tf_op jit(solution)/shard_map/two_orders/pallas_call | solution.py:302
  97.9 5.4 %collective-permute-start.17 = (bf16[18,128,128]{2,1,0:T(8,128)(2,1)S(1)}, bf16[18,128,128]{2,1,0:T(8,128)(2,1)S(1)}, u32[]{:S(2)}, u32[]{:S(2)}) collective-permute-start(bf16[18,128,128]{2,1,0:T(8,128)(2,1)S(1)} %get-tuple-element.53), channel_id=1, source_target_pairs={{0,250},{1,2},{2,1},{3,9},{4,7},{5,255},{6,12},{7,4},{8,11},{9,3},... | collective-permute-start | bytes 1769480 | tf_op jit(solution)/shard_map/ppermute | solution.py:351
  104.3 6.5 %collective-permute-done.17.outer = bf16[18,128,128]{2,1,0:T(8,128)(2,1)S(1)} collective-permute-done((bf16[18,128,128]{2,1,0:T(8,128)(2,1)S(1)}, bf16[18,128,128]{2,1,0:T(8,128)(2,1)S(1)}, u32[]{:S(2)}, u32[]{:S(2)}) %collective-permute-start.17) | collective-permute-done | bytes 589856 | tf_op jit(solution)/shard_map/ppermute | solution.py:351
  110.8 4.2 %two_orders.7 = (bf16[24,128,128]{2,1,0:T(8,128)(2,1)S(1)}, bf16[24,128,128]{2,1,0:T(8,128)(2,1)S(1)}) custom-call(s32[240]{0:T(256)S(1)} %copy-done.2, s32[39]{0:T(128)S(1)} %copy-done.1, bf16[61,128,128]{2,1,0:T(8,128)(2,1)S(1)} %maximum_maximum_fusion.operator, bf16[24,128,128]{2,1,0:T(8,128)(2,1)S(1)} %get-tuple-element.51.own, ...), custom_call_target="tpu_custom_call" | custom-call | flops 2415919104 | bytes 6291456 | tf_op jit(solution)/shard_map/two_orders/pallas_call | solution.py:302
  115.0 3.7 %collective-permute-start.19 = (bf16[24,128,128]{2,1,0:T(8,128)(2,1)S(1)}, bf16[24,128,128]{2,1,0:T(8,128)(2,1)S(1)}, u32[]{:S(2)}, u32[]{:S(2)}) collective-permute-start(bf16[24,128,128]{2,1,0:T(8,128)(2,1)S(1)} %get-tuple-element.58), channel_id=1, source_target_pairs={{0,1},{1,4},{2,3},{3,6},{4,5},{5,0},{6,7},{7,2},{8,13},{9,8},{10,1... | collective-permute-start | bytes 2359304 | tf_op jit(solution)/shard_map/ppermute | solution.py:364
  118.7 1.9 %collective-permute-start.18 = (bf16[24,128,128]{2,1,0:T(8,128)(2,1)S(1)}, bf16[24,128,128]{2,1,0:T(8,128)(2,1)S(1)}, u32[]{:S(2)}, u32[]{:S(2)}) collective-permute-start(bf16[24,128,128]{2,1,0:T(8,128)(2,1)S(1)} %get-tuple-element.57), channel_id=1, source_target_pairs={{0,0},{1,5},{2,2},{3,7},{4,4},{5,1},{6,6},{7,3},{8,12},{9,9},{10,1... | collective-permute-start | bytes 2359304 | tf_op jit(solution)/shard_map/ppermute | solution.py:363
  120.6 12.2 %collective-permute-done.19 = bf16[24,128,128]{2,1,0:T(8,128)(2,1)S(1)} collective-permute-done((bf16[24,128,128]{2,1,0:T(8,128)(2,1)S(1)}, bf16[24,128,128]{2,1,0:T(8,128)(2,1)S(1)}, u32[]{:S(2)}, u32[]{:S(2)}) %collective-permute-start.19) | collective-permute-done | bytes 786464 | tf_op jit(solution)/shard_map/ppermute | solution.py:364
  132.8 5.6 %collective-permute-done.18 = bf16[24,128,128]{2,1,0:T(8,128)(2,1)S(1)} collective-permute-done((bf16[24,128,128]{2,1,0:T(8,128)(2,1)S(1)}, bf16[24,128,128]{2,1,0:T(8,128)(2,1)S(1)}, u32[]{:S(2)}, u32[]{:S(2)}) %collective-permute-start.18) | collective-permute-done | bytes 786464 | tf_op jit(solution)/shard_map/ppermute | solution.py:363
  (36 shorter events, 7.7 us)
Async XLA Ops:
  0.0 8.3 %copy-start.6 = (bf16[6,2,128,128]{3,2,1,0:T(8,128)(2,1)S(1)}, bf16[6,2,128,128]{3,2,1,0:T(8,128)(2,1)}, u32[]{:S(2)}) copy-start(bf16[6,2,128,128]{3,2,1,0:T(8,128)(2,1)} %param.4) | copy-start | bytes 1179652
  0.8 4.8 %collective-permute-start = (s32[6,4]{1,0:T(8,128)S(1)}, s32[6,4]{1,0:T(8,128)S(1)}, u32[]{:S(2)}, u32[]{:S(2)}) collective-permute-start(s32[6,4]{1,0:T(8,128)S(1)} %copy.4), channel_id=1, source_target_pairs={{0,5},{1,0},{2,7},{3,2},{4,1},{5,4},{6,3},{7,6},{8,9},{9,12},{10,1... | collective-permute-start | bytes 296 | tf_op jit(solution)/shard_map/ppermute | solution.py:322
  5.6 13.2 %copy-start.3 = (s32[6,4]{1,0:T(8,128)}, s32[6,4]{1,0:T(8,128)S(1)}, u32[]{:S(2)}) copy-start(s32[6,4]{1,0:T(8,128)S(1)} %collective-permute-done.own) | copy-start | bytes 292
  7.6 9.8 %collective-permute-start.5 = (bf16[12,128,128]{2,1,0:T(8,128)(2,1)S(1)}, bf16[12,128,128]{2,1,0:T(8,128)(2,1)}, u32[]{:S(2)}, u32[]{:S(2)}) collective-permute-start(bf16[12,128,128]{2,1,0:T(8,128)(2,1)S(1)} %bitcast.5), channel_id=1, source_target_pairs={{0,1},{1,4},{2,3},{3,6},{4,5},{5,0},{6,7},{7,2},{8,13},{9,8},{10,1... | collective-permute-start | bytes 1179656 | tf_op jit(solution)/shard_map/ppermute | solution.py:331
  8.3 15.4 %collective-permute-start.3 = (bf16[12,128,128]{2,1,0:T(8,128)(2,1)S(1)}, bf16[12,128,128]{2,1,0:T(8,128)(2,1)S(1)}, u32[]{:S(2)}, u32[]{:S(2)}) collective-permute-start(bf16[12,128,128]{2,1,0:T(8,128)(2,1)S(1)} %bitcast.7), channel_id=1, source_target_pairs={{0,0},{1,5},{2,2},{3,7},{4,4},{5,1},{6,6},{7,3},{8,12},{9,9},{10,1... | collective-permute-start | bytes 1179656 | tf_op jit(solution)/shard_map/ppermute | solution.py:328
  11.1 18.1 %collective-permute-start.4 = (bf16[12,128,128]{2,1,0:T(8,128)(2,1)S(1)}, bf16[12,128,128]{2,1,0:T(8,128)(2,1)S(1)}, u32[]{:S(2)}, u32[]{:S(2)}) collective-permute-start(bf16[12,128,128]{2,1,0:T(8,128)(2,1)S(1)} %bitcast.8), channel_id=1, source_target_pairs={{0,5},{1,0},{2,7},{3,2},{4,1},{5,4},{6,3},{7,6},{8,9},{9,12},{10,1... | collective-permute-start | bytes 1179656 | tf_op jit(solution)/shard_map/ppermute | solution.py:327
  11.2 26.4 %collective-permute-start.7 = (bf16[12,128,128]{2,1,0:T(8,128)(2,1)}, bf16[12,128,128]{2,1,0:T(8,128)(2,1)S(1)}, u32[]{:S(2)}, u32[]{:S(2)}) collective-permute-start(bf16[12,128,128]{2,1,0:T(8,128)(2,1)} %bitcast.2), channel_id=1, source_target_pairs={{0,5},{1,0},{2,7},{3,2},{4,1},{5,4},{6,3},{7,6},{8,9},{9,12},{10,1... | collective-permute-start | bytes 1179656 | tf_op jit(solution)/shard_map/ppermute | solution.py:332
  17.4 20.1 %collective-permute-start.6 = (bf16[12,128,128]{2,1,0:T(8,128)(2,1)}, bf16[12,128,128]{2,1,0:T(8,128)(2,1)S(1)}, u32[]{:S(2)}, u32[]{:S(2)}) collective-permute-start(bf16[12,128,128]{2,1,0:T(8,128)(2,1)} %collective-permute-done.5), channel_id=1, source_target_pairs={{0,1},{1,4},{2,3},{3,6},{4,5},{5,0},{6,7},{7,2},{8,13},{9,8},{10,1... | collective-permute-start | bytes 1179656 | tf_op jit(solution)/shard_map/ppermute | solution.py:333
  18.9 20.4 %collective-permute-start.1 = (s32[6,4]{1,0:T(8,128)S(1)}, s32[6,4]{1,0:T(8,128)S(1)}, u32[]{:S(2)}, u32[]{:S(2)}) collective-permute-start(s32[6,4]{1,0:T(8,128)S(1)} %collective-permute-done.own), channel_id=1, source_target_pairs={{0,2},{1,3},{2,0},{3,1},{4,6},{5,7},{6,4},{7,5},{8,10},{9,11},{10,... | collective-permute-start | bytes 296 | tf_op jit(solution)/shard_map/ppermute | solution.py:325
  23.8 15.5 %collective-permute-start.2 = (s32[6,4]{1,0:T(8,128)}, s32[6,4]{1,0:T(8,128)S(1)}, u32[]{:S(2)}, u32[]{:S(2)}) collective-permute-start(s32[6,4]{1,0:T(8,128)} %copy-done.3), channel_id=1, source_target_pairs={{0,250},{1,2},{2,1},{3,9},{4,7},{5,255},{6,12},{7,4},{8,11},{9,3},... | collective-permute-start | bytes 296 | tf_op jit(solution)/shard_map/ppermute | solution.py:326
  29.2 0.6 copy-start
  39.2 7.7 %copy-start.4 = (s32[6,4]{1,0:T(8,128)}, s32[6,4]{1,0:T(8,128)S(1)}, u32[]{:S(2)}) copy-start(s32[6,4]{1,0:T(8,128)S(1)} %collective-permute-done.1.inner) | copy-start | bytes 292
  39.2 7.7 %copy-start.5 = (s32[6,4]{1,0:T(8,128)}, s32[6,4]{1,0:T(8,128)S(1)}, u32[]{:S(2)}) copy-start(s32[6,4]{1,0:T(8,128)S(1)} %collective-permute-done.2.outer) | copy-start | bytes 292
  39.3 13.8 %collective-permute-start.9 = (bf16[18,128,128]{2,1,0:T(8,128)(2,1)}, bf16[18,128,128]{2,1,0:T(8,128)(2,1)}, u32[]{:S(2)}, u32[]{:S(2)}) collective-permute-start(bf16[18,128,128]{2,1,0:T(8,128)(2,1)} %get-tuple-element.41), channel_id=1, source_target_pairs={{0,250},{1,2},{2,1},{3,9},{4,7},{5,255},{6,12},{7,4},{8,11},{9,3},... | collective-permute-start | bytes 1769480 | tf_op jit(solution)/shard_map/ppermute | solution.py:342
  45.2 7.9 %collective-permute-start.8 = (bf16[18,128,128]{2,1,0:T(8,128)(2,1)S(1)}, bf16[18,128,128]{2,1,0:T(8,128)(2,1)}, u32[]{:S(2)}, u32[]{:S(2)}) collective-permute-start(bf16[18,128,128]{2,1,0:T(8,128)(2,1)S(1)} %get-tuple-element.39), channel_id=1, source_target_pairs={{0,2},{1,3},{2,0},{3,1},{4,6},{5,7},{6,4},{7,5},{8,10},{9,11},{10,... | collective-permute-start | bytes 1769480 | tf_op jit(solution)/shard_map/ppermute | solution.py:343
  45.2 9.4 %collective-permute-start.10 = (bf16[18,128,128]{2,1,0:T(8,128)(2,1)}, bf16[18,128,128]{2,1,0:T(8,128)(2,1)S(1)}, u32[]{:S(2)}, u32[]{:S(2)}) collective-permute-start(bf16[18,128,128]{2,1,0:T(8,128)(2,1)} %get-tuple-element.43), channel_id=1, source_target_pairs={{0,2},{1,3},{2,0},{3,1},{4,6},{5,7},{6,4},{7,5},{8,10},{9,11},{10,... | collective-permute-start | bytes 1769480 | tf_op jit(solution)/shard_map/ppermute | solution.py:352
  45.7 13.7 %collective-permute-start.11 = (bf16[18,128,128]{2,1,0:T(8,128)(2,1)}, bf16[18,128,128]{2,1,0:T(8,128)(2,1)}, u32[]{:S(2)}, u32[]{:S(2)}) collective-permute-start(bf16[18,128,128]{2,1,0:T(8,128)(2,1)} %get-tuple-element.44), channel_id=1, source_target_pairs={{0,250},{1,2},{2,1},{3,9},{4,7},{5,255},{6,12},{7,4},{8,11},{9,3},... | collective-permute-start | bytes 1769480 | tf_op jit(solution)/shard_map/ppermute | solution.py:351
  53.1 6.3 %copy-start.1 = (s32[39]{0:T(128)S(1)}, s32[39]{0:T(128)}, u32[]{:S(2)}) copy-start(s32[39]{0:T(128)} %make_pack.1.pack) | copy-start | bytes 472
  53.1 6.3 %copy-start.2 = (s32[240]{0:T(256)S(1)}, s32[240]{0:T(256)}, u32[]{:S(2)}) copy-start(s32[240]{0:T(256)} %make_table.1.table) | copy-start | bytes 2884
  64.2 5.4 %collective-permute-start.12 = (bf16[18,128,128]{2,1,0:T(8,128)(2,1)S(1)}, bf16[18,128,128]{2,1,0:T(8,128)(2,1)S(1)}, u32[]{:S(2)}, u32[]{:S(2)}) collective-permute-start(bf16[18,128,128]{2,1,0:T(8,128)(2,1)S(1)} %get-tuple-element.46), channel_id=1, source_target_pairs={{0,2},{1,3},{2,0},{3,1},{4,6},{5,7},{6,4},{7,5},{8,10},{9,11},{10,... | collective-permute-start | bytes 1769480 | tf_op jit(solution)/shard_map/ppermute | solution.py:352
  64.5 12.7 %collective-permute-start.13 = (bf16[18,128,128]{2,1,0:T(8,128)(2,1)S(1)}, bf16[18,128,128]{2,1,0:T(8,128)(2,1)S(1)}, u32[]{:S(2)}, u32[]{:S(2)}) collective-permute-start(bf16[18,128,128]{2,1,0:T(8,128)(2,1)S(1)} %get-tuple-element.47), channel_id=1, source_target_pairs={{0,250},{1,2},{2,1},{3,9},{4,7},{5,255},{6,12},{7,4},{8,11},{9,3},... | collective-permute-start | bytes 1769480 | tf_op jit(solution)/shard_map/ppermute | solution.py:351
  81.1 5.2 %collective-permute-start.14 = (bf16[18,128,128]{2,1,0:T(8,128)(2,1)S(1)}, bf16[18,128,128]{2,1,0:T(8,128)(2,1)S(1)}, u32[]{:S(2)}, u32[]{:S(2)}) collective-permute-start(bf16[18,128,128]{2,1,0:T(8,128)(2,1)S(1)} %get-tuple-element.49), channel_id=1, source_target_pairs={{0,2},{1,3},{2,0},{3,1},{4,6},{5,7},{6,4},{7,5},{8,10},{9,11},{10,... | collective-permute-start | bytes 1769480 | tf_op jit(solution)/shard_map/ppermute | solution.py:352
  81.2 12.7 %collective-permute-start.15 = (bf16[18,128,128]{2,1,0:T(8,128)(2,1)S(1)}, bf16[18,128,128]{2,1,0:T(8,128)(2,1)S(1)}, u32[]{:S(2)}, u32[]{:S(2)}) collective-permute-start(bf16[18,128,128]{2,1,0:T(8,128)(2,1)S(1)} %get-tuple-element.50), channel_id=1, source_target_pairs={{0,250},{1,2},{2,1},{3,9},{4,7},{5,255},{6,12},{7,4},{8,11},{9,3},... | collective-permute-start | bytes 1769480 | tf_op jit(solution)/shard_map/ppermute | solution.py:351
  97.8 6.5 %collective-permute-start.16 = (bf16[18,128,128]{2,1,0:T(8,128)(2,1)S(1)}, bf16[18,128,128]{2,1,0:T(8,128)(2,1)S(1)}, u32[]{:S(2)}, u32[]{:S(2)}) collective-permute-start(bf16[18,128,128]{2,1,0:T(8,128)(2,1)S(1)} %get-tuple-element.52), channel_id=1, source_target_pairs={{0,2},{1,3},{2,0},{3,1},{4,6},{5,7},{6,4},{7,5},{8,10},{9,11},{10,... | collective-permute-start | bytes 1769480 | tf_op jit(solution)/shard_map/ppermute | solution.py:352
  97.9 12.9 %collective-permute-start.17 = (bf16[18,128,128]{2,1,0:T(8,128)(2,1)S(1)}, bf16[18,128,128]{2,1,0:T(8,128)(2,1)S(1)}, u32[]{:S(2)}, u32[]{:S(2)}) collective-permute-start(bf16[18,128,128]{2,1,0:T(8,128)(2,1)S(1)} %get-tuple-element.53), channel_id=1, source_target_pairs={{0,250},{1,2},{2,1},{3,9},{4,7},{5,255},{6,12},{7,4},{8,11},{9,3},... | collective-permute-start | bytes 1769480 | tf_op jit(solution)/shard_map/ppermute | solution.py:351
  115.0 17.8 %collective-permute-start.19 = (bf16[24,128,128]{2,1,0:T(8,128)(2,1)S(1)}, bf16[24,128,128]{2,1,0:T(8,128)(2,1)S(1)}, u32[]{:S(2)}, u32[]{:S(2)}) collective-permute-start(bf16[24,128,128]{2,1,0:T(8,128)(2,1)S(1)} %get-tuple-element.58), channel_id=1, source_target_pairs={{0,1},{1,4},{2,3},{3,6},{4,5},{5,0},{6,7},{7,2},{8,13},{9,8},{10,1... | collective-permute-start | bytes 2359304 | tf_op jit(solution)/shard_map/ppermute | solution.py:364
  118.7 19.7 %collective-permute-start.18 = (bf16[24,128,128]{2,1,0:T(8,128)(2,1)S(1)}, bf16[24,128,128]{2,1,0:T(8,128)(2,1)S(1)}, u32[]{:S(2)}, u32[]{:S(2)}) collective-permute-start(bf16[24,128,128]{2,1,0:T(8,128)(2,1)S(1)} %get-tuple-element.57), channel_id=1, source_target_pairs={{0,0},{1,5},{2,2},{3,7},{4,4},{5,1},{6,6},{7,3},{8,12},{9,9},{10,1... | collective-permute-start | bytes 2359304 | tf_op jit(solution)/shard_map/ppermute | solution.py:363
